TPU v7x, 128 devices: a whole 4x4x4 slice. The times are simulated.
128 devices in a mesh: gx: 8 (over x, core), gy: 16 (over y, z).
Axes of the slice: x: 4, y: 4, z: 4, core: 2. Of those that a mesh axis runs over, the one named last changes fastest.
Arguments:
- pressure_source: float32 [128, 512, 256], P('gx', 'gy'), may hold values from -6 to 6
- conductance: float32 [128, 512, 256], P('gx', 'gy'), may hold values from 0.1 to 10
- coarse_inverse: bfloat16 [8, 32, 128, 128], P('gx', 'gy'), may hold values from -4 to 4
Outputs:
- pressure_correction: float32 [128, 512, 256], P('gx', 'gy')
All inputs are finite; a program needn't handle non-finite values.
Results may differ from a plain program's by a relative error of at most 0.0024.
Values may be sent and summed in bfloat16 or wider, within the bound.
A program may use at most 128 MiB of HBM per device.

v0:
```python
import jax
import jax.numpy as jnp
from jax import lax
from jax.sharding import PartitionSpec as P

DEG = 3
LEVELS = 4


LMAX = 2.0
LMIN = 0.25


def with_halo(cells, sides, width):
    for axis, dim in sides:
        count = lax.axis_size(axis)
        ends = count - 1
        head = lax.slice_in_dim(cells, 0, width, axis=dim)
        tail = lax.slice_in_dim(cells, cells.shape[dim] - width, cells.shape[dim], axis=dim)
        cells = jnp.concatenate(
            [
                lax.ppermute(tail, axis, [(i, (i + 1) % count) for i in range(ends)]),
                cells,
                lax.ppermute(head, axis, [((i + 1) % count, i) for i in range(ends)]),
            ],
            axis=dim,
        )
    return cells


def chebyshev_bounds():
    theta = 0.5 * (LMAX + LMIN)
    delta = 0.5 * (LMAX - LMIN)
    return (theta, delta, theta / delta)


def shift_upward(array):
    return jnp.concatenate([array[:, :, 1:], jnp.zeros_like(array[:, :, :1])], axis=2)


def shift_downward(array):
    return jnp.concatenate([jnp.zeros_like(array[:, :, :1]), array[:, :, :-1]], axis=2)


def crop(array, have, want):
    shave = have - want
    if shave == 0:
        return array
    return array[shave : array.shape[0] - shave, shave : array.shape[1] - shave]


def extend(field, width):
    return with_halo(field, (("gx", 0), ("gy", 1)), width)


def setup(kappa_level, margin, scale):
    padded = with_halo(kappa_level.astype(jnp.bfloat16), (("gx", 0), ("gy", 1)), margin + 1).astype(
        kappa_level.dtype
    )
    center = padded[1:-1, 1:-1]
    couplings = (
        0.5 * (center + padded[2:, 1:-1]),
        0.5 * (center + padded[:-2, 1:-1]),
        0.5 * (center + padded[1:-1, 2:]),
        0.5 * (center + padded[1:-1, :-2]),
        0.5 * (center + shift_upward(center)),
        0.5 * (center + shift_downward(center)),
    )
    diagonal = scale * (
        couplings[0] + couplings[1] + couplings[2] + couplings[3] + couplings[4] + couplings[5]
    )
    length_first = kappa_level.shape[0]
    length_second = kappa_level.shape[1]
    places_first = (
        lax.axis_index("gx") * length_first
        + jnp.arange(length_first + 2 * margin, dtype=jnp.int32)
        - margin
    )
    places_second = (
        lax.axis_index("gy") * length_second
        + jnp.arange(length_second + 2 * margin, dtype=jnp.int32)
        - margin
    )
    inside_first = (places_first >= 0) & (places_first < length_first * lax.axis_size("gx"))
    inside_second = (places_second >= 0) & (places_second < length_second * lax.axis_size("gy"))
    inside = inside_first[:, None, None] & inside_second[None, :, None]
    inverse_diagonal = jnp.where(inside, 1.0 / jnp.where(inside, diagonal, 1.0), 0.0)
    return (couplings, inverse_diagonal)


def apply_operator(field, field_margin, couplings, coupling_margin, scale):
    want = field_margin - 1
    trimmed = [crop(coupling, coupling_margin, want) for coupling in couplings]
    center = field[1:-1, 1:-1]
    flux = trimmed[0] * (center - field[2:, 1:-1]) + trimmed[1] * (center - field[:-2, 1:-1])
    flux = flux + trimmed[2] * (center - field[1:-1, 2:]) + trimmed[3] * (center - field[1:-1, :-2])
    flux = (
        flux
        + trimmed[4] * (center - shift_upward(center))
        + trimmed[5] * (center - shift_downward(center))
    )
    return scale * flux


def smooth(
    field,
    field_margin,
    source,
    source_margin,
    couplings,
    coupling_margin,
    inverse_diagonal,
    scale,
    zero_start,
):
    theta, delta, sigma = chebyshev_bounds()
    if zero_start:
        margin_now = source_margin
        update = crop(inverse_diagonal, coupling_margin, margin_now) * source
    else:
        field = extend(field, 1)
        field_margin = 1
        image = apply_operator(field, field_margin, couplings, coupling_margin, scale)
        margin_now = field_margin - 1
        update = crop(inverse_diagonal, coupling_margin, margin_now) * (
            crop(source, source_margin, margin_now) - image
        )
        field = crop(field, field_margin, margin_now)
    direction = update / theta
    ratio = 1.0 / sigma
    for sweep in range(DEG - 1):
        field = direction if field is None else field + direction
        field = extend(field, 1)
        wide_margin = 1
        image = apply_operator(field, wide_margin, couplings, coupling_margin, scale)
        next_margin = wide_margin - 1
        update = crop(inverse_diagonal, coupling_margin, next_margin) * (
            crop(source, source_margin, next_margin) - image
        )
        ratio_next = 1.0 / (2.0 * sigma - ratio)
        direction = (
            ratio_next * ratio * crop(direction, margin_now, next_margin)
            + 2.0 * ratio_next / delta * update
        )
        field = crop(field, wide_margin, next_margin)
        margin_now = next_margin
        ratio = ratio_next
    field = field + direction
    return (field, margin_now)


def restrict(array):
    first, second, third = array.shape
    return array.reshape(first // 2, 2, second // 2, 2, third // 2, 2).mean(axis=(1, 3, 5))


def prolong(array):
    first, second, third = array.shape
    wide = jnp.broadcast_to(array[:, None, :, None, :, None], (first, 2, second, 2, third, 2))
    return wide.reshape(2 * first, 2 * second, 2 * third)


def coarse_solve(source, coarse_inverse):
    slab, local_second, coarse_z = source.shape
    groups = lax.axis_size("gy")
    layers = coarse_z // groups
    whole_second = local_second * groups
    inverses = coarse_inverse[0]
    rounded = source.astype(jnp.bfloat16)
    everything = lax.all_gather(rounded, "gy", axis=1, tiled=True)
    owned = lax.dynamic_slice_in_dim(everything, lax.axis_index("gy") * layers, layers, 2)
    blocks = jnp.transpose(owned, (2, 0, 1)).reshape(layers, slab * whole_second)
    solved = jnp.einsum("kij,kj->ki", inverses, blocks, preferred_element_type=jnp.float32)
    answer = jnp.transpose(solved.reshape(layers, slab, whole_second), (1, 2, 0))
    collected = lax.all_gather(answer, "gy", axis=2, tiled=True)
    return lax.dynamic_slice_in_dim(collected, lax.axis_index("gy") * local_second, local_second, 1)


def local(pressure_source, conductance, coarse_inverse):
    margin = 0
    source = pressure_source
    kappa_level = conductance
    saved = []
    for level in range(LEVELS - 1):
        scale = 0.25**level
        couplings, inverse_diagonal = setup(kappa_level, margin, scale)
        wide_source = source
        field, field_margin = smooth(
            None, 0, wide_source, margin, couplings, margin, inverse_diagonal, scale, True
        )
        field = extend(field, 1)
        field_margin = 1
        residual = crop(wide_source, margin, 0) - apply_operator(
            field, field_margin, couplings, margin, scale
        )
        saved.append(
            (wide_source, crop(field, field_margin, 1)[1:-1, 1:-1], couplings, inverse_diagonal)
        )
        source = restrict(residual)
        kappa_level = restrict(kappa_level)
    correction = coarse_solve(source, coarse_inverse)
    for level in reversed(range(LEVELS - 1)):
        scale = 0.25**level
        wide_source, field, couplings, inverse_diagonal = saved[level]
        field = field + prolong(correction)
        field_margin = 0
        correction, final_margin = smooth(
            field,
            field_margin,
            wide_source,
            margin,
            couplings,
            margin,
            inverse_diagonal,
            scale,
            False,
        )
    return correction


def solution(mesh):
    in_specs = (P("gx", "gy", None), P("gx", "gy", None), P("gx", "gy", None, None))
    out_specs = P("gx", "gy", None)
    return jax.shard_map(local, mesh=mesh, in_specs=in_specs, out_specs=out_specs, check_vma=False)
```

profile of v0, /device:TPU:10, one launch (start us, length us, event | category | flops | bytes accessed | tf_op | source)
XLA Modules:
  0.0 585.1 jit_solution(12494763876065230970)
XLA Ops:
  3.1 3.8 collective-permute-start.1
  6.8 35.6 %reshape.172 = f32[8,2,16,2,128,2]{5,4,3,2,1,0:T(8,128)} reshape(f32[16,32,256]{2,1,0:T(8,128)} %param.4) | data formatting | bytes 1048576 | tf_op jit(solution)/shard_map/reshape | solution.py:154
  42.4 12.2 %reduce_sum.45 = f32[8,16,128]{2,1,0:T(8,128)S(1)} reduce(f32[8,2,16,2,128,2]{5,4,3,2,1,0:T(8,128)} %reshape.172, f32[]{:T(128)} %constant.34.clone.1), dimensions={1,3,5}, to_apply=%region_0.1 | reduce | flops 114688 | bytes 589828 | tf_op jit(solution)/shard_map/reduce_sum | solution.py:154
  56.6 3.6 collective-permute-start.13
  60.2 5.6 div.65
  71.2 3.8 collective-permute-start.2
  75.0 4.1 collective-permute-start.3
  91.2 5.2 collective-permute-start.6
  98.5 6.0 %collective-permute-start.15 = (bf16[10,1,128]{2,1,0:T(2,128)(2,1)S(1)}, bf16[10,1,128]{2,1,0:T(2,128)(2,1)S(1)}, u32[]{:S(2)}, u32[]{:S(2)}) collective-permute-start(bf16[10,1,128]{2,1,0:T(2,128)(2,1)S(1)} %get-tuple-element.117), channel_id=1, source_target_pairs={{1,0},{2,1},{3,2},{4,3},{5,4},{6,5},{7,6},{8,7},{9,8},{10,9},{11,1... | collective-permute-start | bytes 7688 | tf_op jit(solution)/shard_map/ppermute | solution.py:24
  115.0 3.6 collective-permute-start.11
  118.9 3.9 collective-permute-done.11
  134.4 3.9 collective-permute-start.19
  138.5 3.6 collective-permute-done.19
  143.6 35.6 %reshape.173 = f32[8,2,16,2,128,2]{5,4,3,2,1,0:T(8,128)} reshape(f32[16,32,256]{2,1,0:T(8,128)} %fusion.55) | data formatting | bytes 1048576 | tf_op jit(solution)/shard_map/reshape | solution.py:154
  179.2 12.2 %reduce_sum.46 = f32[8,16,128]{2,1,0:T(8,128)S(1)} reduce(f32[8,2,16,2,128,2]{5,4,3,2,1,0:T(8,128)} %reshape.173, f32[]{:T(128)} %constant.34.clone.1), dimensions={1,3,5}, to_apply=%region_1.2 | reduce | flops 114688 | bytes 589828 | tf_op jit(solution)/shard_map/reduce_sum | solution.py:154
  199.8 6.0 %collective-permute-start.31 = (bf16[6,1,64]{2,1,0:T(2,128)(2,1)S(1)}, bf16[6,1,64]{2,1,0:T(2,128)(2,1)S(1)}, u32[]{:S(2)}, u32[]{:S(2)}) collective-permute-start(bf16[6,1,64]{2,1,0:T(2,128)(2,1)S(1)} %get-tuple-element.157), channel_id=1, source_target_pairs={{1,0},{2,1},{3,2},{4,3},{5,4},{6,5},{7,6},{8,7},{9,8},{10,9},{11,1... | collective-permute-start | bytes 2312 | tf_op jit(solution)/shard_map/ppermute | solution.py:24
  207.8 3.9 collective-permute-start.23
  211.8 3.6 collective-permute-done.23
  224.4 4.1 collective-permute-start.27
  241.1 3.9 collective-permute-start.35
  245.1 3.6 collective-permute-done.35
  249.4 6.3 %reshape.174 = f32[4,2,8,2,64,2]{5,4,3,2,1,0:T(8,128)} reshape(f32[8,16,128]{2,1,0:T(8,128)} %fusion.163) | data formatting | bytes 131072 | tf_op jit(solution)/shard_map/reshape | solution.py:154
  268.2 3.9 collective-permute-start.39
  272.2 3.6 collective-permute-done.39
  285.3 3.9 collective-permute-start.43
  289.3 3.6 collective-permute-done.43
  304.1 3.9 collective-permute-start.47
  317.9 21.8 %all_gather.6 = bf16[2,64,32]{2,0,1:T(2,128)(2,1)S(1)} all-gather(bf16[2,4,32]{2,0,1:T(2,128)(2,1)S(1)} %copy.7), channel_id=1, replica_groups=mesh['gx'=8,'gy'=16] {'gy'}, dimensions={1}, use_global_device_ids=true | all-gather | bytes 8704 | tf_op jit(solution)/shard_map/all_gather | solution.py:170
  345.5 22.4 %all_gather.7 = f32[2,64,32]{1,0,2:T(2,128)S(1)} all-gather(f32[2,64,2]{1,0,2:T(2,128)} %bitcast.15), channel_id=1, replica_groups=mesh['gx'=8,'gy'=16] {'gy'}, dimensions={2}, use_global_device_ids=true | all-gather | bytes 17408 | tf_op jit(solution)/shard_map/all_gather | solution.py:175
  381.2 4.6 collective-permute-start.50
  387.8 5.6 collective-permute-done.51
  403.1 3.9 collective-permute-start.55
  420.4 3.9 collective-permute-start.59
  431.5 4.5 reshape.179
  445.7 3.9 collective-permute-start.63
  449.8 3.6 collective-permute-done.63
  463.2 3.9 collective-permute-start.67
  467.2 3.6 collective-permute-done.67
  480.7 3.9 collective-permute-start.71
  484.7 3.6 collective-permute-done.71
  489.4 11.4 %broadcast_in_dim.80 = f32[8,2,16,2,128,2]{5,4,3,2,1,0:T(8,128)} broadcast(f32[8,16,128]{2,1,0:T(8,128)S(1)} %fusion.114), dimensions={0,2,4} | broadcast | bytes 589824 | tf_op jit(solution)/shard_map/broadcast_in_dim | solution.py:159
  500.8 24.6 %reshape.180 = f32[16,32,256]{2,1,0:T(8,128)} reshape(f32[8,2,16,2,128,2]{5,4,3,2,1,0:T(8,128)} %broadcast_in_dim.80) | data formatting | bytes 1048576 | tf_op jit(solution)/shard_map/reshape | solution.py:160
  535.8 3.9 collective-permute-start.75
  539.9 3.6 collective-permute-done.75
  554.5 4.1 collective-permute-start.79
  573.3 3.9 collective-permute-start.83
  577.5 3.6 collective-permute-done.83
  581.1 4.0 fusion.9
  (287 shorter events, 241.7 us)
Async XLA Ops:
  1.1 70.0 %collective-permute-start = (bf16[1,32,256]{2,1,0:T(8,128)(2,1)S(1)}, bf16[1,32,256]{2,1,0:T(8,128)(2,1)S(1)}, u32[]{:S(2)}, u32[]{:S(2)}) collective-permute-start(bf16[1,32,256]{2,1,0:T(8,128)(2,1)S(1)} %get-tuple-element.72), channel_id=1, source_target_pairs={{0,16},{16,32},{32,48},{48,64},{64,80},{80,96},{96,112},{1,17},{17... | collective-permute-start | bytes 49160 | tf_op jit(solution)/shard_map/ppermute | solution.py:22
  3.1 68.1 %collective-permute-start.1 = (bf16[1,32,256]{2,1,0:T(8,128)(2,1)S(1)}, bf16[1,32,256]{2,1,0:T(8,128)(2,1)S(1)}, u32[]{:S(2)}, u32[]{:S(2)}) collective-permute-start(bf16[1,32,256]{2,1,0:T(8,128)(2,1)S(1)} %get-tuple-element.73), channel_id=1, source_target_pairs={{16,0},{32,16},{48,32},{64,48},{80,64},{96,80},{112,96},{17,1},{33... | collective-permute-start | bytes 49160 | tf_op jit(solution)/shard_map/ppermute | solution.py:24
  54.7 31.3 %collective-permute-start.12 = (bf16[1,16,128]{2,1,0:T(8,128)(2,1)S(1)}, bf16[1,16,128]{2,1,0:T(8,128)(2,1)S(1)}, u32[]{:S(2)}, u32[]{:S(2)}) collective-permute-start(bf16[1,16,128]{2,1,0:T(8,128)(2,1)S(1)} %get-tuple-element.118), channel_id=1, source_target_pairs={{0,16},{16,32},{32,48},{48,64},{64,80},{80,96},{96,112},{1,17},{17... | collective-permute-start | bytes 12296 | tf_op jit(solution)/shard_map/ppermute | solution.py:22
  56.6 31.8 %collective-permute-start.13 = (bf16[1,16,128]{2,1,0:T(8,128)(2,1)S(1)}, bf16[1,16,128]{2,1,0:T(8,128)(2,1)S(1)}, u32[]{:S(2)}, u32[]{:S(2)}) collective-permute-start(bf16[1,16,128]{2,1,0:T(8,128)(2,1)S(1)} %get-tuple-element.119), channel_id=1, source_target_pairs={{16,0},{32,16},{48,32},{64,48},{80,64},{96,80},{112,96},{17,1},{33... | collective-permute-start | bytes 12296 | tf_op jit(solution)/shard_map/ppermute | solution.py:24
  69.0 128.1 %collective-permute-start.28 = (bf16[1,8,64]{2,1,0:T(8,128)(2,1)}, bf16[1,8,64]{2,1,0:T(8,128)(2,1)S(1)}, u32[]{:S(2)}, u32[]{:S(2)}) collective-permute-start(bf16[1,8,64]{2,1,0:T(8,128)(2,1)} %get-tuple-element.158), channel_id=1, source_target_pairs={{0,16},{16,32},{32,48},{48,64},{64,80},{80,96},{96,112},{1,17},{17... | collective-permute-start | bytes 3080 | tf_op jit(solution)/shard_map/ppermute | solution.py:22
  71.2 8.6 %collective-permute-start.2 = (bf16[18,1,256]{2,1,0:T(2,128)(2,1)S(1)}, bf16[18,1,256]{2,1,0:T(2,128)(2,1)S(1)}, u32[]{:S(2)}, u32[]{:S(2)}) collective-permute-start(bf16[18,1,256]{2,1,0:T(2,128)(2,1)S(1)} %get-tuple-element.70), channel_id=1, source_target_pairs={{0,1},{1,2},{2,3},{3,4},{4,5},{5,6},{6,7},{7,8},{8,9},{9,10},{10,1... | collective-permute-start | bytes 27656 | tf_op jit(solution)/shard_map/ppermute | solution.py:22
  75.0 7.9 %collective-permute-start.3 = (bf16[18,1,256]{2,1,0:T(2,128)(2,1)S(1)}, bf16[18,1,256]{2,1,0:T(2,128)(2,1)S(1)}, u32[]{:S(2)}, u32[]{:S(2)}) collective-permute-start(bf16[18,1,256]{2,1,0:T(2,128)(2,1)S(1)} %get-tuple-element.71), channel_id=1, source_target_pairs={{1,0},{2,1},{3,2},{4,3},{5,4},{6,5},{7,6},{8,7},{9,8},{10,9},{11,1... | collective-permute-start | bytes 27656 | tf_op jit(solution)/shard_map/ppermute | solution.py:24
  79.7 117.3 %collective-permute-start.29 = (bf16[1,8,64]{2,1,0:T(8,128)(2,1)}, bf16[1,8,64]{2,1,0:T(8,128)(2,1)}, u32[]{:S(2)}, u32[]{:S(2)}) collective-permute-start(bf16[1,8,64]{2,1,0:T(8,128)(2,1)} %get-tuple-element.159), channel_id=1, source_target_pairs={{16,0},{32,16},{48,32},{64,48},{80,64},{96,80},{112,96},{17,1},{33... | collective-permute-start | bytes 3080 | tf_op jit(solution)/shard_map/ppermute | solution.py:24
  84.0 6.3 %collective-permute-start.4 = (f32[1,32,256]{2,1,0:T(8,128)S(1)}, f32[1,32,256]{2,1,0:T(8,128)S(1)}, u32[]{:S(2)}, u32[]{:S(2)}) collective-permute-start(f32[1,32,256]{2,1,0:T(8,128)S(1)} %get-tuple-element.67), channel_id=1, source_target_pairs={{16,0},{32,16},{48,32},{64,48},{80,64},{96,80},{112,96},{17,1},{33... | collective-permute-start | bytes 98312 | tf_op jit(solution)/shard_map/ppermute | solution.py:24
  88.4 19.2 %collective-permute-start.14 = (bf16[10,1,128]{2,1,0:T(2,128)(2,1)S(1)}, bf16[10,1,128]{2,1,0:T(2,128)(2,1)S(1)}, u32[]{:S(2)}, u32[]{:S(2)}) collective-permute-start(bf16[10,1,128]{2,1,0:T(2,128)(2,1)S(1)} %get-tuple-element.116), channel_id=1, source_target_pairs={{0,1},{1,2},{2,3},{3,4},{4,5},{5,6},{6,7},{7,8},{8,9},{9,10},{10,1... | collective-permute-start | bytes 7688 | tf_op jit(solution)/shard_map/ppermute | solution.py:22
  91.2 7.4 %collective-permute-start.6 = (f32[18,1,256]{2,1,0:T(1,128)S(1)}, f32[18,1,256]{2,1,0:T(1,128)S(1)}, u32[]{:S(2)}, u32[]{:S(2)}) collective-permute-start(f32[18,1,256]{2,1,0:T(1,128)S(1)} %get-tuple-element.44), channel_id=1, source_target_pairs={{1,0},{2,1},{3,2},{4,3},{5,4},{6,5},{7,6},{8,7},{9,8},{10,9},{11,1... | collective-permute-start | bytes 55304 | tf_op jit(solution)/shard_map/ppermute | solution.py:24
  96.4 8.2 %collective-permute-start.7 = (f32[18,1,256]{2,1,0:T(1,128)S(1)}, f32[18,1,256]{2,1,0:T(1,128)S(1)}, u32[]{:S(2)}, u32[]{:S(2)}) collective-permute-start(f32[18,1,256]{2,1,0:T(1,128)S(1)} %get-tuple-element.45), channel_id=1, source_target_pairs={{0,1},{1,2},{2,3},{3,4},{4,5},{5,6},{6,7},{7,8},{8,9},{9,10},{10,1... | collective-permute-start | bytes 55304 | tf_op jit(solution)/shard_map/ppermute | solution.py:22
  98.5 11.3 %collective-permute-start.15 = (bf16[10,1,128]{2,1,0:T(2,128)(2,1)S(1)}, bf16[10,1,128]{2,1,0:T(2,128)(2,1)S(1)}, u32[]{:S(2)}, u32[]{:S(2)}) collective-permute-start(bf16[10,1,128]{2,1,0:T(2,128)(2,1)S(1)} %get-tuple-element.117), channel_id=1, source_target_pairs={{1,0},{2,1},{3,2},{4,3},{5,4},{6,5},{7,6},{8,7},{9,8},{10,9},{11,1... | collective-permute-start | bytes 7688 | tf_op jit(solution)/shard_map/ppermute | solution.py:24
  112.8 6.1 %collective-permute-start.10 = (f32[18,1,256]{2,1,0:T(1,128)S(1)}, f32[18,1,256]{2,1,0:T(1,128)S(1)}, u32[]{:S(2)}, u32[]{:S(2)}) collective-permute-start(f32[18,1,256]{2,1,0:T(1,128)S(1)} %get-tuple-element.42), channel_id=1, source_target_pairs={{1,0},{2,1},{3,2},{4,3},{5,4},{6,5},{7,6},{8,7},{9,8},{10,9},{11,1... | collective-permute-start | bytes 55304 | tf_op jit(solution)/shard_map/ppermute | solution.py:24
  115.0 7.8 %collective-permute-start.11 = (f32[18,1,256]{2,1,0:T(1,128)S(1)}, f32[18,1,256]{2,1,0:T(1,128)S(1)}, u32[]{:S(2)}, u32[]{:S(2)}) collective-permute-start(f32[18,1,256]{2,1,0:T(1,128)S(1)} %get-tuple-element.43), channel_id=1, source_target_pairs={{0,1},{1,2},{2,3},{3,4},{4,5},{5,6},{6,7},{7,8},{8,9},{9,10},{10,1... | collective-permute-start | bytes 55304 | tf_op jit(solution)/shard_map/ppermute | solution.py:22
  132.4 6.1 %collective-permute-start.18 = (f32[18,1,256]{2,1,0:T(1,128)S(1)}, f32[18,1,256]{2,1,0:T(1,128)S(1)}, u32[]{:S(2)}, u32[]{:S(2)}) collective-permute-start(f32[18,1,256]{2,1,0:T(1,128)S(1)} %get-tuple-element.40), channel_id=1, source_target_pairs={{1,0},{2,1},{3,2},{4,3},{5,4},{6,5},{7,6},{8,7},{9,8},{10,9},{11,1... | collective-permute-start | bytes 55304 | tf_op jit(solution)/shard_map/ppermute | solution.py:24
  134.4 7.8 %collective-permute-start.19 = (f32[18,1,256]{2,1,0:T(1,128)S(1)}, f32[18,1,256]{2,1,0:T(1,128)S(1)}, u32[]{:S(2)}, u32[]{:S(2)}) collective-permute-start(f32[18,1,256]{2,1,0:T(1,128)S(1)} %get-tuple-element.41), channel_id=1, source_target_pairs={{0,1},{1,2},{2,3},{3,4},{4,5},{5,6},{6,7},{7,8},{8,9},{9,10},{10,1... | collective-permute-start | bytes 55304 | tf_op jit(solution)/shard_map/ppermute | solution.py:22
  192.7 13.1 %collective-permute-start.20 = (f32[1,16,128]{2,1,0:T(8,128)S(1)}, f32[1,16,128]{2,1,0:T(8,128)S(1)}, u32[]{:S(2)}, u32[]{:S(2)}) collective-permute-start(f32[1,16,128]{2,1,0:T(8,128)S(1)} %get-tuple-element.111), channel_id=1, source_target_pairs={{16,0},{32,16},{48,32},{64,48},{80,64},{96,80},{112,96},{17,1},{33... | collective-permute-start | bytes 24584 | tf_op jit(solution)/shard_map/ppermute | solution.py:24
  194.6 11.2 %collective-permute-start.21 = (f32[1,16,128]{2,1,0:T(8,128)S(1)}, f32[1,16,128]{2,1,0:T(8,128)S(1)}, u32[]{:S(2)}, u32[]{:S(2)}) collective-permute-start(f32[1,16,128]{2,1,0:T(8,128)S(1)} %get-tuple-element.110), channel_id=1, source_target_pairs={{0,16},{16,32},{32,48},{48,64},{64,80},{80,96},{96,112},{1,17},{17... | collective-permute-start | bytes 24584 | tf_op jit(solution)/shard_map/ppermute | solution.py:22
  197.9 22.0 %collective-permute-start.30 = (bf16[6,1,64]{2,1,0:T(2,128)(2,1)S(1)}, bf16[6,1,64]{2,1,0:T(2,128)(2,1)S(1)}, u32[]{:S(2)}, u32[]{:S(2)}) collective-permute-start(bf16[6,1,64]{2,1,0:T(2,128)(2,1)S(1)} %get-tuple-element.156), channel_id=1, source_target_pairs={{0,1},{1,2},{2,3},{3,4},{4,5},{5,6},{6,7},{7,8},{8,9},{9,10},{10,1... | collective-permute-start | bytes 2312 | tf_op jit(solution)/shard_map/ppermute | solution.py:22
  199.8 20.1 %collective-permute-start.31 = (bf16[6,1,64]{2,1,0:T(2,128)(2,1)S(1)}, bf16[6,1,64]{2,1,0:T(2,128)(2,1)S(1)}, u32[]{:S(2)}, u32[]{:S(2)}) collective-permute-start(bf16[6,1,64]{2,1,0:T(2,128)(2,1)S(1)} %get-tuple-element.157), channel_id=1, source_target_pairs={{1,0},{2,1},{3,2},{4,3},{5,4},{6,5},{7,6},{8,7},{9,8},{10,9},{11,1... | collective-permute-start | bytes 2312 | tf_op jit(solution)/shard_map/ppermute | solution.py:24
  205.9 5.9 %collective-permute-start.22 = (f32[10,1,128]{2,1,0:T(1,128)S(1)}, f32[10,1,128]{2,1,0:T(1,128)S(1)}, u32[]{:S(2)}, u32[]{:S(2)}) collective-permute-start(f32[10,1,128]{2,1,0:T(1,128)S(1)} %get-tuple-element.86), channel_id=1, source_target_pairs={{1,0},{2,1},{3,2},{4,3},{5,4},{6,5},{7,6},{8,7},{9,8},{10,9},{11,1... | collective-permute-start | bytes 15368 | tf_op jit(solution)/shard_map/ppermute | solution.py:24
  207.8 7.6 %collective-permute-start.23 = (f32[10,1,128]{2,1,0:T(1,128)S(1)}, f32[10,1,128]{2,1,0:T(1,128)S(1)}, u32[]{:S(2)}, u32[]{:S(2)}) collective-permute-start(f32[10,1,128]{2,1,0:T(1,128)S(1)} %get-tuple-element.87), channel_id=1, source_target_pairs={{0,1},{1,2},{2,3},{3,4},{4,5},{5,6},{6,7},{7,8},{8,9},{9,10},{10,1... | collective-permute-start | bytes 15368 | tf_op jit(solution)/shard_map/ppermute | solution.py:22
  222.5 6.1 %collective-permute-start.26 = (f32[10,1,128]{2,1,0:T(1,128)S(1)}, f32[10,1,128]{2,1,0:T(1,128)S(1)}, u32[]{:S(2)}, u32[]{:S(2)}) collective-permute-start(f32[10,1,128]{2,1,0:T(1,128)S(1)} %get-tuple-element.84), channel_id=1, source_target_pairs={{1,0},{2,1},{3,2},{4,3},{5,4},{6,5},{7,6},{8,7},{9,8},{10,9},{11,1... | collective-permute-start | bytes 15368 | tf_op jit(solution)/shard_map/ppermute | solution.py:24
  224.4 7.6 %collective-permute-start.27 = (f32[10,1,128]{2,1,0:T(1,128)S(1)}, f32[10,1,128]{2,1,0:T(1,128)S(1)}, u32[]{:S(2)}, u32[]{:S(2)}) collective-permute-start(f32[10,1,128]{2,1,0:T(1,128)S(1)} %get-tuple-element.85), channel_id=1, source_target_pairs={{0,1},{1,2},{2,3},{3,4},{4,5},{5,6},{6,7},{7,8},{8,9},{9,10},{10,1... | collective-permute-start | bytes 15368 | tf_op jit(solution)/shard_map/ppermute | solution.py:22
  239.2 5.9 %collective-permute-start.34 = (f32[10,1,128]{2,1,0:T(1,128)S(1)}, f32[10,1,128]{2,1,0:T(1,128)S(1)}, u32[]{:S(2)}, u32[]{:S(2)}) collective-permute-start(f32[10,1,128]{2,1,0:T(1,128)S(1)} %get-tuple-element.82), channel_id=1, source_target_pairs={{1,0},{2,1},{3,2},{4,3},{5,4},{6,5},{7,6},{8,7},{9,8},{10,9},{11,1... | collective-permute-start | bytes 15368 | tf_op jit(solution)/shard_map/ppermute | solution.py:24
  241.1 7.6 %collective-permute-start.35 = (f32[10,1,128]{2,1,0:T(1,128)S(1)}, f32[10,1,128]{2,1,0:T(1,128)S(1)}, u32[]{:S(2)}, u32[]{:S(2)}) collective-permute-start(f32[10,1,128]{2,1,0:T(1,128)S(1)} %get-tuple-element.83), channel_id=1, source_target_pairs={{0,1},{1,2},{2,3},{3,4},{4,5},{5,6},{6,7},{7,8},{8,9},{9,10},{10,1... | collective-permute-start | bytes 15368 | tf_op jit(solution)/shard_map/ppermute | solution.py:22
  266.2 5.9 %collective-permute-start.38 = (f32[6,1,64]{2,1,0:T(1,128)S(1)}, f32[6,1,64]{2,1,0:T(1,128)S(1)}, u32[]{:S(2)}, u32[]{:S(2)}) collective-permute-start(f32[6,1,64]{2,1,0:T(1,128)S(1)} %get-tuple-element.130), channel_id=1, source_target_pairs={{1,0},{2,1},{3,2},{4,3},{5,4},{6,5},{7,6},{8,7},{9,8},{10,9},{11,1... | collective-permute-start | bytes 4616 | tf_op jit(solution)/shard_map/ppermute | solution.py:24
  268.2 7.6 %collective-permute-start.39 = (f32[6,1,64]{2,1,0:T(1,128)S(1)}, f32[6,1,64]{2,1,0:T(1,128)S(1)}, u32[]{:S(2)}, u32[]{:S(2)}) collective-permute-start(f32[6,1,64]{2,1,0:T(1,128)S(1)} %get-tuple-element.131), channel_id=1, source_target_pairs={{0,1},{1,2},{2,3},{3,4},{4,5},{5,6},{6,7},{7,8},{8,9},{9,10},{10,1... | collective-permute-start | bytes 4616 | tf_op jit(solution)/shard_map/ppermute | solution.py:22
  285.3 7.6 %collective-permute-start.43 = (f32[6,1,64]{2,1,0:T(1,128)S(1)}, f32[6,1,64]{2,1,0:T(1,128)S(1)}, u32[]{:S(2)}, u32[]{:S(2)}) collective-permute-start(f32[6,1,64]{2,1,0:T(1,128)S(1)} %get-tuple-element.129), channel_id=1, source_target_pairs={{0,1},{1,2},{2,3},{3,4},{4,5},{5,6},{6,7},{7,8},{8,9},{9,10},{10,1... | collective-permute-start | bytes 4616 | tf_op jit(solution)/shard_map/ppermute | solution.py:22
  302.2 6.7 %collective-permute-start.46 = (f32[6,1,64]{2,1,0:T(1,128)S(1)}, f32[6,1,64]{2,1,0:T(1,128)S(1)}, u32[]{:S(2)}, u32[]{:S(2)}) collective-permute-start(f32[6,1,64]{2,1,0:T(1,128)S(1)} %get-tuple-element.126), channel_id=1, source_target_pairs={{1,0},{2,1},{3,2},{4,3},{5,4},{6,5},{7,6},{8,7},{9,8},{10,9},{11,1... | collective-permute-start | bytes 4616 | tf_op jit(solution)/shard_map/ppermute | solution.py:24
  304.1 7.6 %collective-permute-start.47 = (f32[6,1,64]{2,1,0:T(1,128)S(1)}, f32[6,1,64]{2,1,0:T(1,128)S(1)}, u32[]{:S(2)}, u32[]{:S(2)}) collective-permute-start(f32[6,1,64]{2,1,0:T(1,128)S(1)} %get-tuple-element.127), channel_id=1, source_target_pairs={{0,1},{1,2},{2,3},{3,4},{4,5},{5,6},{6,7},{7,8},{8,9},{9,10},{10,1... | collective-permute-start | bytes 4616 | tf_op jit(solution)/shard_map/ppermute | solution.py:22
  381.2 6.6 %collective-permute-start.50 = (f32[6,1,64]{2,1,0:T(1,128)S(1)}, f32[6,1,64]{2,1,0:T(1,128)S(1)}, u32[]{:S(2)}, u32[]{:S(2)}) collective-permute-start(f32[6,1,64]{2,1,0:T(1,128)S(1)} %get-tuple-element.124), channel_id=1, source_target_pairs={{1,0},{2,1},{3,2},{4,3},{5,4},{6,5},{7,6},{8,7},{9,8},{10,9},{11,1... | collective-permute-start | bytes 4616 | tf_op jit(solution)/shard_map/ppermute | solution.py:24
  385.8 7.6 %collective-permute-start.51 = (f32[6,1,64]{2,1,0:T(1,128)S(1)}, f32[6,1,64]{2,1,0:T(1,128)S(1)}, u32[]{:S(2)}, u32[]{:S(2)}) collective-permute-start(f32[6,1,64]{2,1,0:T(1,128)S(1)} %get-tuple-element.125), channel_id=1, source_target_pairs={{0,1},{1,2},{2,3},{3,4},{4,5},{5,6},{6,7},{7,8},{8,9},{9,10},{10,1... | collective-permute-start | bytes 4616 | tf_op jit(solution)/shard_map/ppermute | solution.py:22
  403.1 7.6 %collective-permute-start.55 = (f32[6,1,64]{2,1,0:T(1,128)S(1)}, f32[6,1,64]{2,1,0:T(1,128)S(1)}, u32[]{:S(2)}, u32[]{:S(2)}) collective-permute-start(f32[6,1,64]{2,1,0:T(1,128)S(1)} %get-tuple-element.123), channel_id=1, source_target_pairs={{0,1},{1,2},{2,3},{3,4},{4,5},{5,6},{6,7},{7,8},{8,9},{9,10},{10,1... | collective-permute-start | bytes 4616 | tf_op jit(solution)/shard_map/ppermute | solution.py:22
  420.4 7.6 %collective-permute-start.59 = (f32[6,1,64]{2,1,0:T(1,128)S(1)}, f32[6,1,64]{2,1,0:T(1,128)S(1)}, u32[]{:S(2)}, u32[]{:S(2)}) collective-permute-start(f32[6,1,64]{2,1,0:T(1,128)S(1)} %get-tuple-element.121), channel_id=1, source_target_pairs={{0,1},{1,2},{2,3},{3,4},{4,5},{5,6},{6,7},{7,8},{8,9},{9,10},{10,1... | collective-permute-start | bytes 4616 | tf_op jit(solution)/shard_map/ppermute | solution.py:22
  443.8 5.9 %collective-permute-start.62 = (f32[10,1,128]{2,1,0:T(1,128)S(1)}, f32[10,1,128]{2,1,0:T(1,128)S(1)}, u32[]{:S(2)}, u32[]{:S(2)}) collective-permute-start(f32[10,1,128]{2,1,0:T(1,128)S(1)} %get-tuple-element.80), channel_id=1, source_target_pairs={{1,0},{2,1},{3,2},{4,3},{5,4},{6,5},{7,6},{8,7},{9,8},{10,9},{11,1... | collective-permute-start | bytes 15368 | tf_op jit(solution)/shard_map/ppermute | solution.py:24
  445.7 7.6 %collective-permute-start.63 = (f32[10,1,128]{2,1,0:T(1,128)S(1)}, f32[10,1,128]{2,1,0:T(1,128)S(1)}, u32[]{:S(2)}, u32[]{:S(2)}) collective-permute-start(f32[10,1,128]{2,1,0:T(1,128)S(1)} %get-tuple-element.81), channel_id=1, source_target_pairs={{0,1},{1,2},{2,3},{3,4},{4,5},{5,6},{6,7},{7,8},{8,9},{9,10},{10,1... | collective-permute-start | bytes 15368 | tf_op jit(solution)/shard_map/ppermute | solution.py:22
  461.3 5.9 %collective-permute-start.66 = (f32[10,1,128]{2,1,0:T(1,128)S(1)}, f32[10,1,128]{2,1,0:T(1,128)S(1)}, u32[]{:S(2)}, u32[]{:S(2)}) collective-permute-start(f32[10,1,128]{2,1,0:T(1,128)S(1)} %get-tuple-element.78), channel_id=1, source_target_pairs={{1,0},{2,1},{3,2},{4,3},{5,4},{6,5},{7,6},{8,7},{9,8},{10,9},{11,1... | collective-permute-start | bytes 15368 | tf_op jit(solution)/shard_map/ppermute | solution.py:24
  463.2 7.6 %collective-permute-start.67 = (f32[10,1,128]{2,1,0:T(1,128)S(1)}, f32[10,1,128]{2,1,0:T(1,128)S(1)}, u32[]{:S(2)}, u32[]{:S(2)}) collective-permute-start(f32[10,1,128]{2,1,0:T(1,128)S(1)} %get-tuple-element.79), channel_id=1, source_target_pairs={{0,1},{1,2},{2,3},{3,4},{4,5},{5,6},{6,7},{7,8},{8,9},{9,10},{10,1... | collective-permute-start | bytes 15368 | tf_op jit(solution)/shard_map/ppermute | solution.py:22
  478.8 5.9 %collective-permute-start.70 = (f32[10,1,128]{2,1,0:T(1,128)S(1)}, f32[10,1,128]{2,1,0:T(1,128)S(1)}, u32[]{:S(2)}, u32[]{:S(2)}) collective-permute-start(f32[10,1,128]{2,1,0:T(1,128)S(1)} %get-tuple-element.76), channel_id=1, source_target_pairs={{1,0},{2,1},{3,2},{4,3},{5,4},{6,5},{7,6},{8,7},{9,8},{10,9},{11,1... | collective-permute-start | bytes 15368 | tf_op jit(solution)/shard_map/ppermute | solution.py:24
  480.7 7.6 %collective-permute-start.71 = (f32[10,1,128]{2,1,0:T(1,128)S(1)}, f32[10,1,128]{2,1,0:T(1,128)S(1)}, u32[]{:S(2)}, u32[]{:S(2)}) collective-permute-start(f32[10,1,128]{2,1,0:T(1,128)S(1)} %get-tuple-element.77), channel_id=1, source_target_pairs={{0,1},{1,2},{2,3},{3,4},{4,5},{5,6},{6,7},{7,8},{8,9},{9,10},{10,1... | collective-permute-start | bytes 15368 | tf_op jit(solution)/shard_map/ppermute | solution.py:22
  533.8 6.1 %collective-permute-start.74 = (f32[18,1,256]{2,1,0:T(1,128)S(1)}, f32[18,1,256]{2,1,0:T(1,128)S(1)}, u32[]{:S(2)}, u32[]{:S(2)}) collective-permute-start(f32[18,1,256]{2,1,0:T(1,128)S(1)} %get-tuple-element.38), channel_id=1, source_target_pairs={{1,0},{2,1},{3,2},{4,3},{5,4},{6,5},{7,6},{8,7},{9,8},{10,9},{11,1... | collective-permute-start | bytes 55304 | tf_op jit(solution)/shard_map/ppermute | solution.py:24
  535.8 7.8 %collective-permute-start.75 = (f32[18,1,256]{2,1,0:T(1,128)S(1)}, f32[18,1,256]{2,1,0:T(1,128)S(1)}, u32[]{:S(2)}, u32[]{:S(2)}) collective-permute-start(f32[18,1,256]{2,1,0:T(1,128)S(1)} %get-tuple-element.39), channel_id=1, source_target_pairs={{0,1},{1,2},{2,3},{3,4},{4,5},{5,6},{6,7},{7,8},{8,9},{9,10},{10,1... | collective-permute-start | bytes 55304 | tf_op jit(solution)/shard_map/ppermute | solution.py:22
  552.6 6.3 %collective-permute-start.78 = (f32[18,1,256]{2,1,0:T(1,128)S(1)}, f32[18,1,256]{2,1,0:T(1,128)S(1)}, u32[]{:S(2)}, u32[]{:S(2)}) collective-permute-start(f32[18,1,256]{2,1,0:T(1,128)S(1)} %get-tuple-element.36), channel_id=1, source_target_pairs={{1,0},{2,1},{3,2},{4,3},{5,4},{6,5},{7,6},{8,7},{9,8},{10,9},{11,1... | collective-permute-start | bytes 55304 | tf_op jit(solution)/shard_map/ppermute | solution.py:24
  554.5 7.8 %collective-permute-start.79 = (f32[18,1,256]{2,1,0:T(1,128)S(1)}, f32[18,1,256]{2,1,0:T(1,128)S(1)}, u32[]{:S(2)}, u32[]{:S(2)}) collective-permute-start(f32[18,1,256]{2,1,0:T(1,128)S(1)} %get-tuple-element.37), channel_id=1, source_target_pairs={{0,1},{1,2},{2,3},{3,4},{4,5},{5,6},{6,7},{7,8},{8,9},{9,10},{10,1... | collective-permute-start | bytes 55304 | tf_op jit(solution)/shard_map/ppermute | solution.py:22
  571.4 6.1 %collective-permute-start.82 = (f32[18,1,256]{2,1,0:T(1,128)S(1)}, f32[18,1,256]{2,1,0:T(1,128)S(1)}, u32[]{:S(2)}, u32[]{:S(2)}) collective-permute-start(f32[18,1,256]{2,1,0:T(1,128)S(1)} %get-tuple-element.34), channel_id=1, source_target_pairs={{1,0},{2,1},{3,2},{4,3},{5,4},{6,5},{7,6},{8,7},{9,8},{10,9},{11,1... | collective-permute-start | bytes 55304 | tf_op jit(solution)/shard_map/ppermute | solution.py:24
  573.3 7.8 %collective-permute-start.83 = (f32[18,1,256]{2,1,0:T(1,128)S(1)}, f32[18,1,256]{2,1,0:T(1,128)S(1)}, u32[]{:S(2)}, u32[]{:S(2)}) collective-permute-start(f32[18,1,256]{2,1,0:T(1,128)S(1)} %get-tuple-element.35), channel_id=1, source_target_pairs={{0,1},{1,2},{2,3},{3,4},{4,5},{5,6},{6,7},{7,8},{8,9},{9,10},{10,1... | collective-permute-start | bytes 55304 | tf_op jit(solution)/shard_map/ppermute | solution.py:22
  (55 other events, 1330.3 us)
where the time goes:
time: 590 us; the launch traced here: 585 us
  starting transfers between devices  226 us (38%)
  local copies, waits for them, and re-layouts  144 us (24%)
  waiting for transfers between devices  103 us (17%)
  other arithmetic  64.7 us (11%)
  blocking collectives  44.2 us (7%)
    ppermute x42, starting transfers between devices, with_halo(): lax.ppermute(tail, axis, [(i, (i + 1) % count) for i in range(ends)])  123 us
    ppermute x42, waiting for transfers between devices, with_halo(): lax.ppermute(tail, axis, [(i, (i + 1) % count) for i in range(ends)])  103 us
    ppermute x42, starting transfers between devices, with_halo(): lax.ppermute(head, axis, [((i + 1) % count, i) for i in range(ends)])  102 us
    reshape x4, local copies, waits for them, and re-layouts, restrict(): array.reshape(first // 2, 2, second // 2, 2, third // 2, 2)  79.5 us
    reduce_sum x5, other arithmetic, restrict(): array.reshape(first // 2, 2, second // 2, 2, third // 2, 2)  31.2 us
    reshape x3, local copies, waits for them, and re-layouts, prolong(): return wide.reshape(2 * first, 2 * second, 2 * third)  31 us
    all_gather x1, blocking collectives, coarse_solve(): collected = lax.all_gather(answer, 'gy', axis=2, tiled=True)  22.4 us
    all_gather x1, blocking collectives, coarse_solve(): everything = lax.all_gather(rounded, 'gy', axis=1, tiled=True)  21.8 us
  transfers between devices with their start and end apart: 84, of which 34 were waited for; matrix products, arithmetic and copies ran while one was open for 20% of the time, Pallas kernels for 0%

commit v1 on v0

v1 whole, which is shorter than its diff:
```python
import functools

import jax
import jax.numpy as jnp
from jax import lax
from jax.experimental import pallas as pl
from jax.experimental.pallas import tpu as pltpu
from jax.sharding import PartitionSpec as P

MESH = pl.DeviceIdType.MESH

LMAX = 2.0
LMIN = 0.25
THETA = 0.5 * (LMAX + LMIN)
DELTA = 0.5 * (LMAX - LMIN)
SIGMA = THETA / DELTA
RATIO_0 = 1.0 / SIGMA
RATIO_1 = 1.0 / (2.0 * SIGMA - RATIO_0)
RATIO_2 = 1.0 / (2.0 * SIGMA - RATIO_1)
STEP_1 = (RATIO_1 * RATIO_0, 2.0 * RATIO_1 / DELTA)
STEP_2 = (RATIO_2 * RATIO_1, 2.0 * RATIO_2 / DELTA)

F32 = jnp.float32
BF16 = jnp.bfloat16

AROUND = [(a, b) for a in (-1, 0, 1) for b in (-1, 0, 1) if (a, b) != (0, 0)]
WIDE = [(a, b) for a in (-2, -1, 0, 1, 2) for b in (-1, 0, 1) if (a, b) != (0, 0)]


class Level:
    def __init__(self, nx, ny, X, x0, R, J, hold, row0, erow, xc):
        self.nx, self.ny, self.X, self.x0, self.R, self.J = nx, ny, X, x0, R, J
        self.hold, self.row0, self.erow, self.xc = hold, row0, erow, xc
        self.rows = 16 + ny

    def scratch(self, coarse_x):
        X, R, J = self.X, self.R, self.J
        vm = lambda *shape: pltpu.VMEM(shape + (128,), F32)
        return dict(
            NS=vm(X, R, self.rows),
            NK=vm(X, R, self.rows),
            NV=vm(X, R, self.rows),
            SV=vm(self.nx + 2, R, self.rows),
            RN=vm(self.nx, R, self.rows),
            E=vm(coarse_x, R, 2 * (self.ny // 2 + 16) if self.nx > 4 else 24),
            HK=vm(X, R, J + 2, 8),
            CX=vm(X + 1, R, J, 8),
            CY=vm(X, R, J + 1, 8),
            CM=vm(X, R, J, 8),
            CP=vm(X, R, J, 8),
            Q=vm(X, R, J, 8),
            G=vm(X, R, J, 8),
            D=vm(X, R, J, 8),
            DIR=vm(X, R, J, 8),
            VA=vm(X, R, J + 2, 8),
            VB=vm(X, R, J + 2, 8),
        )


LEVELS = (
    Level(16, 32, 24, 4, 2, 5, 1, 4, 12, 6),
    Level(8, 16, 24, 8, 1, 4, 1, 0, 8, 4),
    Level(4, 8, 20, 8, 1, 3, 2, 0, 0, 0),
)
COARSE_X = (24, 20, 10)


def lanes():
    return lax.broadcasted_iota(jnp.int32, (8, 128), 1)


def sublanes():
    return lax.broadcasted_iota(jnp.int32, (8, 128), 0)


def turn(value, shift, axis):
    return pltpu.roll(value, shift % value.shape[axis], axis)


def pick(value, index):
    return jnp.take_along_axis(value, index, axis=1, mode="promise_in_bounds")


def rows_of(L, j):
    return pl.ds(L.row0 + j, 8, stride=L.J)


def beside_z(L, parts):
    h = L.hold
    down = [turn(p, h, 1) for p in parts]
    up = [turn(p, -h, 1) for p in parts]
    if L.R == 2:
        lane = lanes()
        down[1] = jnp.where(lane == 0, down[0], down[1])
        up[0] = jnp.where(lane == 127, up[1], up[0])
    return down, up


def store_wrapped(ref, x, r, J, values):
    for j in range(J):
        ref[x, r, j + 1] = values[j]
    ref[x, r, 0] = turn(values[J - 1], 1, 0)
    ref[x, r, J + 1] = turn(values[0], -1, 0)


def loop(lo, hi, body):
    def step(x, carry):
        body(x)
        return carry

    lax.fori_loop(lo, hi, step, 0)


def prepare(L, M, lo, hi, gx, gy, count_x, count_y):
    J, R = L.J, L.R
    sub, lane = sublanes(), lanes()
    first = gy * L.ny - 8 + L.row0
    keep = []
    for j in range(J):
        place = first + j + J * sub
        keep.append(jnp.where((place >= 0) & (place < L.ny * count_y), 0.5, 0.0).astype(F32))

    def halves(x):
        place = gx * L.nx + x - L.x0
        inside = jnp.where((place >= 0) & (place < L.nx * count_x), 1.0, 0.0).astype(F32)
        for r in range(R):
            store_wrapped(M["HK"], x, r, J, [M["NK"][x, r, rows_of(L, j), :] * (keep[j] * inside) for j in range(J)])

    loop(lo - 1, hi + 1, halves)
    HK = M["HK"]
    for r in range(R):
        for j in range(J):
            M["CX"][lo, r, j] = HK[lo - 1, r, j + 1] + HK[lo, r, j + 1]

    def couple(x):
        for j in range(J):
            mine = [HK[x, r, j + 1] for r in range(R)]
            down, up = beside_z(L, mine)
            down[0] = jnp.where(lane < L.hold, 0.0, down[0])
            up[R - 1] = jnp.where(lane >= 128 - L.hold, 0.0, up[R - 1])
            for r in range(R):
                h = mine[r]
                xm, xp = HK[x - 1, r, j + 1], HK[x + 1, r, j + 1]
                ym, yp = HK[x, r, j], HK[x, r, j + 2]
                diagonal = (xm + xp) + (ym + yp) + (down[r] + up[r]) + 6.0 * h
                M["CX"][x + 1, r, j] = h + xp
                M["CY"][x, r, j] = h + ym
                if j == J - 1:
                    M["CY"][x, r, J] = h + yp
                low, high = h + down[r], h + up[r]
                if r == 0:
                    low = jnp.where(lane < L.hold, 0.0, low)
                if r == R - 1:
                    high = jnp.where(lane >= 128 - L.hold, 0.0, high)
                M["CM"][x, r, j] = low
                M["CP"][x, r, j] = high
                M["D"][x, r, j] = diagonal
                M["Q"][x, r, j] = jnp.where(h > 0.0, 1.0 / diagonal, 0.0)

    loop(lo, hi, couple)


def scale_source(L, M, lo, hi, start):
    J = L.J

    def body(x):
        for r in range(L.R):
            values = []
            for j in range(J):
                g = M["Q"][x, r, j] * M["NS"][x, r, rows_of(L, j), :]
                M["G"][x, r, j] = g
                values.append(g * (1.0 / THETA))
            if start:
                store_wrapped(M["VA"], x, r, J, values)

    loop(lo, hi, body)


def sweep(L, M, src, dst, lo, hi, kind, step=None, keep_rows=None, emit=None):
    J, R = L.J, L.R
    V = M[src]

    def body(x):
        new = [[None] * J for _ in range(R)]
        for j in range(J):
            mine = [V[x, r, j + 1] for r in range(R)]
            down, up = beside_z(L, mine)
            for r in range(R):
                c = mine[r]
                near = M["CX"][x, r, j] * V[x - 1, r, j + 1] + M["CX"][x + 1, r, j] * V[x + 1, r, j + 1]
                near = near + (M["CY"][x, r, j] * V[x, r, j] + M["CY"][x, r, j + 1] * V[x, r, j + 2])
                near = near + (M["CM"][x, r, j] * down[r] + M["CP"][x, r, j] * up[r])
                update = (M["G"][x, r, j] - c) + M["Q"][x, r, j] * near
                if kind == "residual":
                    M["RN"][x - L.x0, r, rows_of(L, j), :] = M["D"][x, r, j] * update
                    continue
                if kind == "first":
                    direction = update * (1.0 / THETA)
                elif kind == "from_zero":
                    direction = step[0] * c + step[1] * update
                else:
                    direction = step[0] * M["DIR"][x, r, j] + step[1] * update
                if kind != "last":
                    M["DIR"][x, r, j] = direction
                new[r][j] = c + direction
        if kind == "residual":
            return
        for r in range(R):
            if dst is not None:
                store_wrapped(M[dst], x, r, J, new[r])
            if keep_rows is not None:
                for j in range(J):
                    keep_rows[x - L.x0 + 1, r, rows_of(L, j), :] = new[r][j]
        if emit is not None:
            emit(x, new)

    loop(lo, hi, body)


def descend(L, M):
    lo, hi = L.x0, L.x0 + L.nx
    sweep(L, M, "VA", "VB", lo - 2, hi + 2, "from_zero", STEP_1)
    sweep(L, M, "VB", "VA", lo - 1, hi + 1, "last", STEP_2, keep_rows=M["SV"])
    sweep(L, M, "VA", None, lo, hi, "residual")


def ascend(L, M, margin, emit):
    lo, hi = L.x0, L.x0 + L.nx

    def begin(x):
        xc = lax.shift_right_logical(x, 1) + L.xc
        for r in range(L.R):
            values = []
            for j in range(L.J):
                added = M["E"][xc, r, pl.ds(L.erow + j, 8, stride=L.J), :]
                total = M["NV"][x, r, rows_of(L, j), :] + added
                values.append(jnp.where(M["HK"][x, r, j + 1] > 0.0, total, 0.0))
            store_wrapped(M["VA"], x, r, L.J, values)

    loop(lo - margin, hi + margin, begin)
    margin -= 1
    sweep(L, M, "VA", "VB", lo - margin, hi + margin, "first")
    margin -= 1
    sweep(L, M, "VB", "VA", lo - margin, hi + margin, "next", STEP_1)
    margin -= 1
    sweep(L, M, "VA", None, lo - margin, hi + margin, "last", STEP_2, emit=emit)


def coarsen(L, src, sx0, scale, put):
    lane = lanes()
    even = (lane * 2) & 127

    def body(x):
        for t in range(max(1, L.ny // 16)):
            sums = []
            for r in range(L.R):
                rows = [
                    src[sx0 + 2 * x + dx, r, pl.ds(8 + 16 * t + b, 8, stride=2), :] for dx in (0, 1) for b in (0, 1)
                ]
                total = (rows[0] + rows[1]) + (rows[2] + rows[3])
                if L.R == 2:
                    sums.append(pick(total + turn(total, -1, 1), even))
                else:
                    other = jnp.where((lane & L.hold) == 0, turn(total, -L.hold, 1), turn(total, L.hold, 1))
                    sums.append(total + other)
            value = jnp.where(lane < 64, sums[0], sums[1]) if L.R == 2 else sums[0]
            put(x, t, value * scale)

    return body


def coarsen_into(L, src, sx0, scale, nxt, dst):
    def put(x, t, value):
        dst[nxt.x0 + x, 0, 8 + 8 * t : 16 + 8 * t, :] = value

    loop(0, L.nx // 2, coarsen(L, src, sx0, scale, put))


def kernel(gx_size, gy_size, names, source, conductance, inverse, out, *refs):
    S = dict(zip(names, refs))
    M = [{k[1:]: v for k, v in S.items() if k[0] == str(l)} for l in range(3)]
    gx, gy = lax.axis_index("gx"), lax.axis_index("gy")
    L0, L1, L2 = LEVELS

    def device(a, b):
        return {"gx": lax.rem(gx + a + gx_size, gx_size), "gy": lax.rem(gy + b + gy_size, gy_size)}

    def remote(src, dst, name, n, a, b):
        return pltpu.make_async_remote_copy(
            src_ref=src,
            dst_ref=dst,
            send_sem=S["send_" + name].at[n],
            recv_sem=S["recv_" + name].at[n],
            device_id=device(a, b),
            device_id_type=MESH,
        )

    def exchange(L, src, sx0, dst, width, where, name):
        copies = []
        for n, (a, b) in enumerate(where):
            if a == 0:
                xs, xd, wx = sx0, L.x0, L.nx
            elif abs(a) == 2:
                xs, xd, wx = sx0, L.x0 - (a // 2) * 2 * L.nx, L.nx
            elif a == 1:
                xs, xd, wx = sx0 + L.nx - width, L.x0 - width, width
            else:
                xs, xd, wx = sx0, L.x0 + L.nx, width
            if b == 0:
                ys, yd, wy = 8, 8, L.ny
            elif b == 1:
                ys, yd, wy = L.ny, 0, 8
            else:
                ys, yd, wy = 8, 8 + L.ny, 8
            copies.append(
                remote(
                    src.at[pl.ds(xs, wx), :, pl.ds(ys, wy), :],
                    dst.at[pl.ds(xd, wx), :, pl.ds(yd, wy), :],
                    name,
                    n,
                    a,
                    b,
                )
            )
        for copy in copies:
            copy.start()
        return copies

    def arrive(copies):
        for copy in copies:
            copy.wait_recv()

    sent = []

    peers = list(WIDE) + [(0, b) for b in range(2, gy_size - 1)]
    barrier = pltpu.get_barrier_semaphore()
    for a, b in peers:
        pl.semaphore_signal(barrier, inc=1, device_id=device(a, b), device_id_type=MESH)

    loads = []
    for n, (src, dst) in enumerate(((conductance, M[0]["NK"]), (source, M[0]["NS"]))):
        for r in range(2):
            copy = pltpu.make_async_copy(
                src.at[:, :, pl.ds(128 * r, 128)],
                dst.at[pl.ds(4, 16), r, pl.ds(8, 32), :],
                S["local"].at[2 * n + r],
            )
            copy.start()
            loads.append(copy)
    for copy in loads:
        copy.wait()

    sub, lane = sublanes(), lanes()
    XP, YP, XR, YR = S["xp"], S["yp"], S["xr"], S["yr"]
    fields = (M[0]["NK"], M[0]["NS"])

    def pack_x(i):
        for a in range(2):
            for r in range(2):
                XP[0, a, i, r] = fields[a][4 + i, r, 8:40, :].astype(BF16)
                XP[1, a, i, r] = fields[a][16 + i, r, 8:40, :].astype(BF16)

    loop(0, 4, pack_x)

    def pack_y(i):
        for a in range(2):
            low, high = [], []
            for d in range(2):
                x = 4 + 2 * i + d
                near, far = fields[a][x, 0, 8:16, :], fields[a][x, 1, 8:16, :]
                low.append(jnp.where(sub < 4, near, turn(far, 4, 0)))
                near, far = fields[a][x, 0, 32:40, :], fields[a][x, 1, 32:40, :]
                high.append(jnp.where(sub < 4, turn(near, 4, 0), far))
            YP[0, a, i] = jnp.concatenate(low, axis=0).astype(BF16)
            YP[1, a, i] = jnp.concatenate(high, axis=0).astype(BF16)

    loop(0, 8, pack_y)

    pl.semaphore_wait(barrier, len(peers))

    fine = []
    for n, (a, b) in enumerate(AROUND):
        if b == 0:
            fine.append(remote(XP.at[(a + 1) // 2], XR.at[(1 - a) // 2], "fine", n, a, b))
        else:
            xs, xd, wx = {0: (0, 2, 8), 1: (6, 0, 2), -1: (0, 10, 2)}[a]
            fine.append(
                remote(
                    YP.at[(b + 1) // 2, :, pl.ds(xs, wx)],
                    YR.at[(1 - b) // 2, :, pl.ds(xd, wx)],
                    "fine",
                    n,
                    a,
                    b,
                )
            )
    for copy in fine:
        copy.start()
    sent += fine

    coarsen_into(L0, M[0]["NK"], 4, 0.125, L1, M[1]["NK"])
    kappa_1 = exchange(L1, M[1]["NK"], 8, M[1]["NK"], 6, AROUND, "kappa_1")
    coarsen_into(L1, M[1]["NK"], 8, 0.125, L2, M[2]["NK"])
    kappa_2 = exchange(L2, M[2]["NK"], 8, M[2]["NK"], 4, WIDE, "kappa_2")
    sent += kappa_1 + kappa_2

    one = lambda mask: jnp.where(mask, 1.0, 0.0).astype(BF16)
    row = lax.broadcasted_iota(jnp.int32, (128, 128), 0)
    column = lax.broadcasted_iota(jnp.int32, (128, 128), 1)
    order = one(row == ((column >> 2) & 1) * 64 + (column >> 3) * 4 + (column & 3))
    for k in range(2):
        S["mp"][128 * k : 128 * (k + 1), :] = jnp.dot(
            inverse[0, k], order, preferred_element_type=F32
        ).astype(BF16)

    row = lax.broadcasted_iota(jnp.int32, (48, 256), 0)
    column = lax.broadcasted_iota(jnp.int32, (48, 256), 1)
    layer = jnp.where(row >= 24, 1, 0)
    row = row - 24 * layer
    half = jnp.where(row >= 12, 1, 0)
    row = row - 12 * half
    base = layer * 128 + half * 64

    def share(d):
        chosen = one(column == base + ((row + (4 * d + 60)) & 63))
        S["ms"][d] = jnp.dot(chosen, S["mp"][...], preferred_element_type=F32).astype(BF16)

    loop(0, gy_size, share)
    matrices = []
    for n in range(gy_size - 1):
        there = lax.rem(gy + n + 1, gy_size)
        matrices.append(remote(S["ms"].at[there], S["mm"].at[gy], "matrix", n, 0, n + 1))
    for copy in matrices:
        copy.start()
    sent += matrices
    S["mm"][gy] = S["ms"][gy]

    arrive(fine)

    def unpack_x(i):
        for a in range(2):
            for r in range(2):
                fields[a][i, r, 8:40, :] = XR[0, a, i, r].astype(F32)
                fields[a][20 + i, r, 8:40, :] = XR[1, a, i, r].astype(F32)

    loop(0, 4, unpack_x)

    def unpack_y(i):
        for a in range(2):
            low, high = YR[0, a, i].astype(F32), YR[1, a, i].astype(F32)
            for d in range(2):
                x = 2 * i + d
                part = low[8 * d : 8 * d + 8]
                fields[a][x, 0, 0:8, :] = turn(part, 4, 0)
                fields[a][x, 1, 0:8, :] = part
                part = high[8 * d : 8 * d + 8]
                fields[a][x, 0, 40:48, :] = part
                fields[a][x, 1, 40:48, :] = turn(part, 4, 0)

    loop(0, 12, unpack_y)

    place = (gx, gy, gx_size, gy_size)
    prepare(L0, M[0], 1, 23, *place)
    scale_source(L0, M[0], 1, 23, True)
    descend(L0, M[0])
    coarsen_into(L0, M[0]["RN"], 0, 0.5, L1, M[1]["NS"])
    source_1 = exchange(L1, M[1]["NS"], 8, M[1]["NS"], 4, AROUND, "source_1")
    smooth_0 = exchange(L0, M[0]["SV"], 1, M[0]["NV"], 3, AROUND, "smooth_0")
    sent += source_1 + smooth_0

    arrive(kappa_1)
    prepare(L1, M[1], 3, 21, *place)
    arrive(source_1)
    scale_source(L1, M[1], 4, 20, True)
    descend(L1, M[1])
    coarsen_into(L1, M[1]["RN"], 0, 0.5, L2, M[2]["NS"])
    source_2 = exchange(L2, M[2]["NS"], 8, M[2]["NS"], 4, WIDE, "source_2")
    smooth_1 = exchange(L1, M[1]["SV"], 1, M[1]["NV"], 5, AROUND, "smooth_1")
    sent += source_2 + smooth_1

    arrive(kappa_2)
    prepare(L2, M[2], 3, 17, *place)
    arrive(source_2)
    scale_source(L2, M[2], 3, 17, True)
    descend(L2, M[2])
    tiles = []
    make = coarsen(L2, M[2]["RN"], 0, 1.0 / 128.0, lambda x, t, value: tiles.append(value))
    make(0)
    make(1)
    rounded = jnp.where(sub < 4, tiles[0], turn(tiles[1], 4, 0)).astype(BF16).astype(F32)
    S["mine"][...] = rounded
    gathered = []
    for n in range(gy_size - 1):
        gathered.append(remote(S["mine"], S["all"].at[gy], "gather", n, 0, n + 1))
    for copy in gathered:
        copy.start()
    smooth_2 = exchange(L2, M[2]["SV"], 1, M[2]["NV"], 4, WIDE, "smooth_2")
    sent += gathered + smooth_2
    S["all"][gy] = rounded

    kept = []
    for l, L in enumerate(LEVELS):
        copy = pltpu.make_async_copy(
            M[l]["SV"].at[pl.ds(1, L.nx), :, pl.ds(8, L.ny), :],
            M[l]["NV"].at[pl.ds(L.x0, L.nx), :, pl.ds(8, L.ny), :],
            S["local"].at[l],
        )
        copy.start()
        kept.append(copy)
    for copy in kept:
        copy.wait()

    arrive(matrices)
    arrive(gathered)
    right = S["all"][...].reshape(gy_size * 8, 128).astype(BF16)
    layer_of = lax.broadcasted_iota(jnp.int32, (24, 128), 1) >> 2

    def solve(d, total):
        product = jnp.dot(S["mm"][d], right, preferred_element_type=F32)
        total = total + jnp.where(layer_of == 2 * d, product[:24], 0.0)
        return total + jnp.where(layer_of == 2 * d + 1, product[24:], 0.0)

    S["corr"][2] = lax.fori_loop(0, gy_size, solve, jnp.zeros((24, 128), F32))
    coarse = []
    for n, a in enumerate((-2, -1, 1, 2)):
        coarse.append(remote(S["corr"].at[2], S["corr"].at[2 - a], "coarse", n, a, 0))
    for copy in coarse:
        copy.start()
    sent += coarse
    arrive(smooth_2)
    arrive(coarse)

    for slab in range(5):
        for d in range(2):
            for b in range(2):
                M[2]["E"][2 * slab + d, 0, pl.ds(b, 8, stride=2), :] = S["corr"][slab, 12 * d : 12 * d + 8, :]
                M[2]["E"][2 * slab + d, 0, pl.ds(16 + b, 4, stride=2), :] = S["corr"][slab, 12 * d + 8 : 12 * d + 12, :]

    def emit_2(x, new):
        for j in range(L2.J):
            for b in range(2):
                M[1]["E"][x, 0, pl.ds(2 * j + b, 8, stride=2 * L2.J), :] = new[0][j]

    def emit_1(x, new):
        for j in range(L1.J):
            for r in range(2):
                value = pick(new[0][j], (lane >> 1) + 64 * r)
                for b in range(2):
                    M[0]["E"][x, r, pl.ds(2 * j + b, 8, stride=2 * L1.J), :] = value

    def emit_0(x, new):
        for r in range(2):
            for j in range(L0.J):
                S["result"][x - L0.x0, r, rows_of(L0, j), :] = new[r][j]

    ascend(L2, M[2], 6, emit_2)
    arrive(smooth_1)
    ascend(L1, M[1], 5, emit_1)
    arrive(smooth_0)
    ascend(L0, M[0], 3, emit_0)

    stores = []
    for r in range(2):
        copy = pltpu.make_async_copy(
            S["result"].at[:, r, pl.ds(8, 32), :], out.at[:, :, pl.ds(128 * r, 128)], S["local"].at[r]
        )
        copy.start()
        stores.append(copy)
    for copy in sent:
        copy.wait_send()
    for copy in stores:
        copy.wait()


def solution(mesh):
    gx_size, gy_size = mesh.shape["gx"], mesh.shape["gy"]
    scratch = {}
    for l, L in enumerate(LEVELS):
        for name, shape in L.scratch(COARSE_X[l]).items():
            scratch[str(l) + name] = shape
    scratch["xp"] = pltpu.VMEM((2, 2, 4, 2, 32, 128), BF16)
    scratch["xr"] = pltpu.VMEM((2, 2, 4, 2, 32, 128), BF16)
    scratch["yp"] = pltpu.VMEM((2, 2, 8, 16, 128), BF16)
    scratch["yr"] = pltpu.VMEM((2, 2, 12, 16, 128), BF16)
    scratch["mp"] = pltpu.VMEM((256, 128), BF16)
    scratch["ms"] = pltpu.VMEM((gy_size, 48, 128), BF16)
    scratch["mm"] = pltpu.VMEM((gy_size, 48, 128), BF16)
    scratch["mine"] = pltpu.VMEM((8, 128), F32)
    scratch["all"] = pltpu.VMEM((gy_size, 8, 128), F32)
    scratch["corr"] = pltpu.VMEM((5, 24, 128), F32)
    scratch["result"] = pltpu.VMEM((16, 2, 48, 128), F32)
    scratch["local"] = pltpu.SemaphoreType.DMA((4,))
    line = gy_size - 1
    counts = dict(
        fine=8, kappa_1=8, kappa_2=14, matrix=line, source_1=8, smooth_0=8, source_2=14, smooth_1=8,
        gather=line, smooth_2=14, coarse=4,
    )
    for name, count in counts.items():
        scratch["send_" + name] = pltpu.SemaphoreType.DMA((count,))
        scratch["recv_" + name] = pltpu.SemaphoreType.DMA((count,))

    def local(pressure_source, conductance, coarse_inverse):
        return pl.pallas_call(
            functools.partial(kernel, gx_size, gy_size, tuple(scratch)),
            out_shape=jax.ShapeDtypeStruct(pressure_source.shape, F32),
            in_specs=[
                pl.BlockSpec(memory_space=pl.ANY),
                pl.BlockSpec(memory_space=pl.ANY),
                pl.BlockSpec(memory_space=pltpu.VMEM),
            ],
            out_specs=pl.BlockSpec(memory_space=pl.ANY),
            scratch_shapes=list(scratch.values()),
            compiler_params=pltpu.CompilerParams(
                collective_id=0, has_side_effects=True, vmem_limit_bytes=56 * 2**20
            ),
        )(pressure_source, conductance, coarse_inverse)

    in_specs = (P("gx", "gy", None), P("gx", "gy", None), P("gx", "gy", None, None))
    return jax.shard_map(local, mesh=mesh, in_specs=in_specs, out_specs=P("gx", "gy", None), check_vma=False)
```

time: 590 us -> 71.6 us (0.12)
  the two profiles are of different devices: /device:TPU:10 before, /device:TPU:1 now
where the time goes in v1:
time: 71.6 us; the launch traced here: 71.4 us
  Pallas kernels  69.5 us (97%)
  local copies, waits for them, and re-layouts  1.88 us (3%)
    pallas_call x1, Pallas kernels, local(): pl.pallas_call(functools.partial(kernel, gx_size, gy_size, tuple(scratch)...  69.5 us
    unnamed x1, local copies, waits for them, and re-layouts  1.88 us

profile of v1, /device:TPU:1, one launch (start us, length us, event | category | flops | bytes accessed | tf_op | source)
XLA Modules:
  0.0 71.4 jit_solution(1245509186523216431)
XLA Ops:
  0.0 69.5 %shard_map.37 = f32[16,32,256]{2,1,0:T(8,128)} custom-call(f32[16,32,256]{2,1,0:T(8,128)} %source.1, f32[16,32,256]{2,1,0:T(8,128)} %conductance.1, bf16[1,2,128,128]{3,2,1,0:T(8,128)(2,1)} %inverse.1), custom_call_target="tpu_custom_call" | custom-call | tf_op jit(solution)/shard_map/pallas_call | solution.py:603
  69.5 1.9 %copy.5 = f32[16,32,256]{2,1,0:T(8,128)} copy(f32[16,32,256]{2,1,0:T(8,128)} %shard_map.37) | data formatting | bytes 1048576

commit v2 on v1

--- a/solution.py
+++ b/solution.py
@@ -28,10 +28,10 @@
 
 
 class Level:
-    def __init__(self, nx, ny, X, x0, R, J, hold, row0, erow, xc):
+    def __init__(self, nx, ny, X, x0, R, J, hold, row0, erow, xc, most):
         self.nx, self.ny, self.X, self.x0, self.R, self.J = nx, ny, X, x0, R, J
         self.hold, self.row0, self.erow, self.xc = hold, row0, erow, xc
-        self.rows = 16 + ny
+        self.rows, self.most = 16 + ny, most
 
     def scratch(self, coarse_x):
         X, R, J = self.X, self.R, self.J
@@ -58,9 +58,9 @@
 
 
 LEVELS = (
-    Level(16, 32, 24, 4, 2, 5, 1, 4, 12, 6),
-    Level(8, 16, 24, 8, 1, 4, 1, 0, 8, 4),
-    Level(4, 8, 20, 8, 1, 3, 2, 0, 0, 0),
+    Level(16, 32, 24, 4, 2, 5, 1, 4, 12, 6, 6),
+    Level(8, 16, 24, 8, 1, 4, 1, 0, 8, 4, 16),
+    Level(4, 8, 20, 8, 1, 3, 2, 0, 0, 0, 16),
 )
 COARSE_X = (24, 20, 10)
 
@@ -103,12 +103,18 @@
     ref[x, r, J + 1] = turn(values[0], -1, 0)
 
 
-def loop(lo, hi, body):
-    def step(x, carry):
-        body(x)
+def loop(lo, hi, body, most=1):
+    count = hi - lo
+    U = max(u for u in range(1, most + 1) if count % u == 0)
+    if U == count:
+        body(lo, U)
+        return
+
+    def step(i, carry):
+        body(lo + i * U, U)
         return carry
 
-    lax.fori_loop(lo, hi, step, 0)
+    lax.fori_loop(0, count // U, step, 0)
 
 
 def prepare(L, M, lo, hi, gx, gy, count_x, count_y):
@@ -120,101 +126,115 @@
         place = first + j + J * sub
         keep.append(jnp.where((place >= 0) & (place < L.ny * count_y), 0.5, 0.0).astype(F32))
 
-    def halves(x):
-        place = gx * L.nx + x - L.x0
-        inside = jnp.where((place >= 0) & (place < L.nx * count_x), 1.0, 0.0).astype(F32)
-        for r in range(R):
-            store_wrapped(M["HK"], x, r, J, [M["NK"][x, r, rows_of(L, j), :] * (keep[j] * inside) for j in range(J)])
-
-    loop(lo - 1, hi + 1, halves)
-    HK = M["HK"]
+    def halves(x, U):
+        NK, HK = M["NK"].at[pl.ds(x, U)], M["HK"].at[pl.ds(x, U)]
+        for u in range(U):
+            place = gx * L.nx + x + u - L.x0
+            inside = jnp.where((place >= 0) & (place < L.nx * count_x), 1.0, 0.0).astype(F32)
+            for r in range(R):
+                store_wrapped(HK, u, r, J, [NK[u, r, rows_of(L, j), :] * (keep[j] * inside) for j in range(J)])
+
+    loop(lo - 1, hi + 1, halves, L.most)
     for r in range(R):
         for j in range(J):
-            M["CX"][lo, r, j] = HK[lo - 1, r, j + 1] + HK[lo, r, j + 1]
-
-    def couple(x):
-        for j in range(J):
-            mine = [HK[x, r, j + 1] for r in range(R)]
-            down, up = beside_z(L, mine)
-            down[0] = jnp.where(lane < L.hold, 0.0, down[0])
-            up[R - 1] = jnp.where(lane >= 128 - L.hold, 0.0, up[R - 1])
-            for r in range(R):
-                h = mine[r]
-                xm, xp = HK[x - 1, r, j + 1], HK[x + 1, r, j + 1]
-                ym, yp = HK[x, r, j], HK[x, r, j + 2]
-                diagonal = (xm + xp) + (ym + yp) + (down[r] + up[r]) + 6.0 * h
-                M["CX"][x + 1, r, j] = h + xp
-                M["CY"][x, r, j] = h + ym
-                if j == J - 1:
-                    M["CY"][x, r, J] = h + yp
-                low, high = h + down[r], h + up[r]
-                if r == 0:
-                    low = jnp.where(lane < L.hold, 0.0, low)
-                if r == R - 1:
-                    high = jnp.where(lane >= 128 - L.hold, 0.0, high)
-                M["CM"][x, r, j] = low
-                M["CP"][x, r, j] = high
-                M["D"][x, r, j] = diagonal
-                M["Q"][x, r, j] = jnp.where(h > 0.0, 1.0 / diagonal, 0.0)
-
-    loop(lo, hi, couple)
+            M["CX"][lo, r, j] = M["HK"][lo - 1, r, j + 1] + M["HK"][lo, r, j + 1]
+
+    def couple(x, U):
+        HK, CX = M["HK"].at[pl.ds(x - 1, U + 2)], M["CX"].at[pl.ds(x, U + 1)]
+        CY, CM, CP, D, Q = (M[name].at[pl.ds(x, U)] for name in ("CY", "CM", "CP", "D", "Q"))
+        for u in range(U):
+            for j in range(J):
+                mine = [HK[u + 1, r, j + 1] for r in range(R)]
+                down, up = beside_z(L, mine)
+                down[0] = jnp.where(lane < L.hold, 0.0, down[0])
+                up[R - 1] = jnp.where(lane >= 128 - L.hold, 0.0, up[R - 1])
+                for r in range(R):
+                    h = mine[r]
+                    xm, xp = HK[u, r, j + 1], HK[u + 2, r, j + 1]
+                    ym, yp = HK[u + 1, r, j], HK[u + 1, r, j + 2]
+                    diagonal = (xm + xp) + (ym + yp) + (down[r] + up[r]) + 6.0 * h
+                    CX[u + 1, r, j] = h + xp
+                    CY[u, r, j] = h + ym
+                    if j == J - 1:
+                        CY[u, r, J] = h + yp
+                    low, high = h + down[r], h + up[r]
+                    if r == 0:
+                        low = jnp.where(lane < L.hold, 0.0, low)
+                    if r == R - 1:
+                        high = jnp.where(lane >= 128 - L.hold, 0.0, high)
+                    CM[u, r, j] = low
+                    CP[u, r, j] = high
+                    D[u, r, j] = diagonal
+                    Q[u, r, j] = jnp.where(h > 0.0, 1.0 / diagonal, 0.0)
+
+    loop(lo, hi, couple, L.most)
 
 
 def scale_source(L, M, lo, hi, start):
     J = L.J
 
-    def body(x):
-        for r in range(L.R):
-            values = []
-            for j in range(J):
-                g = M["Q"][x, r, j] * M["NS"][x, r, rows_of(L, j), :]
-                M["G"][x, r, j] = g
-                values.append(g * (1.0 / THETA))
-            if start:
-                store_wrapped(M["VA"], x, r, J, values)
-
-    loop(lo, hi, body)
+    def body(x, U):
+        Q, NS, G, VA = (M[name].at[pl.ds(x, U)] for name in ("Q", "NS", "G", "VA"))
+        for u in range(U):
+            for r in range(L.R):
+                values = []
+                for j in range(J):
+                    g = Q[u, r, j] * NS[u, r, rows_of(L, j), :]
+                    G[u, r, j] = g
+                    values.append(g * (1.0 / THETA))
+                if start:
+                    store_wrapped(VA, u, r, J, values)
+
+    loop(lo, hi, body, L.most)
 
 
 def sweep(L, M, src, dst, lo, hi, kind, step=None, keep_rows=None, emit=None):
     J, R = L.J, L.R
-    V = M[src]
-
-    def body(x):
-        new = [[None] * J for _ in range(R)]
-        for j in range(J):
-            mine = [V[x, r, j + 1] for r in range(R)]
-            down, up = beside_z(L, mine)
+
+    def body(x, U):
+        V, CX = M[src].at[pl.ds(x - 1, U + 2)], M["CX"].at[pl.ds(x, U + 1)]
+        CY, CM, CP, D, Q, G, DIR = (M[name].at[pl.ds(x, U)] for name in ("CY", "CM", "CP", "D", "Q", "G", "DIR"))
+        if dst is not None:
+            W = M[dst].at[pl.ds(x, U)]
+        if kind == "residual":
+            RN = M["RN"].at[pl.ds(x - L.x0, U)]
+        if keep_rows is not None:
+            kept = keep_rows.at[pl.ds(x - L.x0 + 1, U)]
+        for u in range(U):
+            new = [[None] * J for _ in range(R)]
+            for j in range(J):
+                mine = [V[u + 1, r, j + 1] for r in range(R)]
+                down, up = beside_z(L, mine)
+                for r in range(R):
+                    c = mine[r]
+                    near = CX[u, r, j] * V[u, r, j + 1] + CX[u + 1, r, j] * V[u + 2, r, j + 1]
+                    near = near + (CY[u, r, j] * V[u + 1, r, j] + CY[u, r, j + 1] * V[u + 1, r, j + 2])
+                    near = near + (CM[u, r, j] * down[r] + CP[u, r, j] * up[r])
+                    update = (G[u, r, j] - c) + Q[u, r, j] * near
+                    if kind == "residual":
+                        RN[u, r, rows_of(L, j), :] = D[u, r, j] * update
+                        continue
+                    if kind == "first":
+                        direction = update * (1.0 / THETA)
+                    elif kind == "from_zero":
+                        direction = step[0] * c + step[1] * update
+                    else:
+                        direction = step[0] * DIR[u, r, j] + step[1] * update
+                    if kind != "last":
+                        DIR[u, r, j] = direction
+                    new[r][j] = c + direction
+            if kind == "residual":
+                continue
             for r in range(R):
-                c = mine[r]
-                near = M["CX"][x, r, j] * V[x - 1, r, j + 1] + M["CX"][x + 1, r, j] * V[x + 1, r, j + 1]
-                near = near + (M["CY"][x, r, j] * V[x, r, j] + M["CY"][x, r, j + 1] * V[x, r, j + 2])
-                near = near + (M["CM"][x, r, j] * down[r] + M["CP"][x, r, j] * up[r])
-                update = (M["G"][x, r, j] - c) + M["Q"][x, r, j] * near
-                if kind == "residual":
-                    M["RN"][x - L.x0, r, rows_of(L, j), :] = M["D"][x, r, j] * update
-                    continue
-                if kind == "first":
-                    direction = update * (1.0 / THETA)
-                elif kind == "from_zero":
-                    direction = step[0] * c + step[1] * update
-                else:
-                    direction = step[0] * M["DIR"][x, r, j] + step[1] * update
-                if kind != "last":
-                    M["DIR"][x, r, j] = direction
-                new[r][j] = c + direction
-        if kind == "residual":
-            return
-        for r in range(R):
-            if dst is not None:
-                store_wrapped(M[dst], x, r, J, new[r])
-            if keep_rows is not None:
-                for j in range(J):
-                    keep_rows[x - L.x0 + 1, r, rows_of(L, j), :] = new[r][j]
-        if emit is not None:
-            emit(x, new)
-
-    loop(lo, hi, body)
+                if dst is not None:
+                    store_wrapped(W, u, r, J, new[r])
+                if keep_rows is not None:
+                    for j in range(J):
+                        kept[u, r, rows_of(L, j), :] = new[r][j]
+            if emit is not None:
+                emit(x + u, new)
+
+    loop(lo, hi, body, L.most)
 
 
 def descend(L, M):
@@ -227,17 +247,19 @@
 def ascend(L, M, margin, emit):
     lo, hi = L.x0, L.x0 + L.nx
 
-    def begin(x):
-        xc = lax.shift_right_logical(x, 1) + L.xc
-        for r in range(L.R):
-            values = []
-            for j in range(L.J):
-                added = M["E"][xc, r, pl.ds(L.erow + j, 8, stride=L.J), :]
-                total = M["NV"][x, r, rows_of(L, j), :] + added
-                values.append(jnp.where(M["HK"][x, r, j + 1] > 0.0, total, 0.0))
-            store_wrapped(M["VA"], x, r, L.J, values)
-
-    loop(lo - margin, hi + margin, begin)
+    def begin(x, U):
+        NV, HK, VA = (M[name].at[pl.ds(x, U)] for name in ("NV", "HK", "VA"))
+        for u in range(U):
+            xc = lax.shift_right_logical(x + u, 1) + L.xc
+            for r in range(L.R):
+                values = []
+                for j in range(L.J):
+                    added = M["E"][xc, r, pl.ds(L.erow + j, 8, stride=L.J), :]
+                    total = NV[u, r, rows_of(L, j), :] + added
+                    values.append(jnp.where(HK[u, r, j + 1] > 0.0, total, 0.0))
+                store_wrapped(VA, u, r, L.J, values)
+
+    loop(lo - margin, hi + margin, begin, L.most)
     margin -= 1
     sweep(L, M, "VA", "VB", lo - margin, hi + margin, "first")
     margin -= 1
@@ -250,13 +272,12 @@
     lane = lanes()
     even = (lane * 2) & 127
 
-    def body(x):
-        for t in range(max(1, L.ny // 16)):
+    def body(x, U):
+        pairs = src.at[pl.ds(sx0 + 2 * x, 2 * U)]
+        for u, t in [(u, t) for u in range(U) for t in range(max(1, L.ny // 16))]:
             sums = []
             for r in range(L.R):
-                rows = [
-                    src[sx0 + 2 * x + dx, r, pl.ds(8 + 16 * t + b, 8, stride=2), :] for dx in (0, 1) for b in (0, 1)
-                ]
+                rows = [pairs[2 * u + dx, r, pl.ds(8 + 16 * t + b, 8, stride=2), :] for dx in (0, 1) for b in (0, 1)]
                 total = (rows[0] + rows[1]) + (rows[2] + rows[3])
                 if L.R == 2:
                     sums.append(pick(total + turn(total, -1, 1), even))
@@ -264,7 +285,7 @@
                     other = jnp.where((lane & L.hold) == 0, turn(total, -L.hold, 1), turn(total, L.hold, 1))
                     sums.append(total + other)
             value = jnp.where(lane < 64, sums[0], sums[1]) if L.R == 2 else sums[0]
-            put(x, t, value * scale)
+            put(x + u, t, value * scale)
 
     return body
 
@@ -273,7 +294,7 @@
     def put(x, t, value):
         dst[nxt.x0 + x, 0, 8 + 8 * t : 16 + 8 * t, :] = value
 
-    loop(0, L.nx // 2, coarsen(L, src, sx0, scale, put))
+    loop(0, L.nx // 2, coarsen(L, src, sx0, scale, put), 4)
 
 
 def kernel(gx_size, gy_size, names, source, conductance, inverse, out, *refs):
@@ -354,7 +375,7 @@
     XP, YP, XR, YR = S["xp"], S["yp"], S["xr"], S["yr"]
     fields = (M[0]["NK"], M[0]["NS"])
 
-    def pack_x(i):
+    def pack_x(i, _):
         for a in range(2):
             for r in range(2):
                 XP[0, a, i, r] = fields[a][4 + i, r, 8:40, :].astype(BF16)
@@ -362,7 +383,7 @@
 
     loop(0, 4, pack_x)
 
-    def pack_y(i):
+    def pack_y(i, _):
         for a in range(2):
             low, high = [], []
             for d in range(2):
@@ -421,7 +442,7 @@
     row = row - 12 * half
     base = layer * 128 + half * 64
 
-    def share(d):
+    def share(d, _):
         chosen = one(column == base + ((row + (4 * d + 60)) & 63))
         S["ms"][d] = jnp.dot(chosen, S["mp"][...], preferred_element_type=F32).astype(BF16)
 
@@ -437,7 +458,7 @@
 
     arrive(fine)
 
-    def unpack_x(i):
+    def unpack_x(i, _):
         for a in range(2):
             for r in range(2):
                 fields[a][i, r, 8:40, :] = XR[0, a, i, r].astype(F32)
@@ -445,7 +466,7 @@
 
     loop(0, 4, unpack_x)
 
-    def unpack_y(i):
+    def unpack_y(i, _):
         for a in range(2):
             low, high = YR[0, a, i].astype(F32), YR[1, a, i].astype(F32)
             for d in range(2):
@@ -485,8 +506,7 @@
     descend(L2, M[2])
     tiles = []
     make = coarsen(L2, M[2]["RN"], 0, 1.0 / 128.0, lambda x, t, value: tiles.append(value))
-    make(0)
-    make(1)
+    make(0, 2)
     rounded = jnp.where(sub < 4, tiles[0], turn(tiles[1], 4, 0)).astype(BF16).astype(F32)
     S["mine"][...] = rounded
     gathered = []

time: 71.6 us -> 53.2 us (0.74)
  Pallas kernels: 69.5 us -> 51.1 us
    pallas_call x1, Pallas kernels: 69.5 us -> 51.1 us  [local(): pl.pallas_call(functools.partial(kernel, gx_size, gy_size, tuple(scratch)...]
where the time goes in v2:
time: 53.2 us; the launch traced here: 53 us
  Pallas kernels  51.1 us (96%)
  local copies, waits for them, and re-layouts  1.88 us (4%)
    pallas_call x1, Pallas kernels, local(): pl.pallas_call(functools.partial(kernel, gx_size, gy_size, tuple(scratch)...  51.1 us
    unnamed x1, local copies, waits for them, and re-layouts  1.88 us

profile of v2, /device:TPU:1, one launch (start us, length us, event | category | flops | bytes accessed | tf_op | source)
XLA Modules:
  0.0 53.0 jit_solution(1545049289549803482)
XLA Ops:
  0.0 51.1 %shard_map.37 = f32[16,32,256]{2,1,0:T(8,128)} custom-call(f32[16,32,256]{2,1,0:T(8,128)} %source.1, f32[16,32,256]{2,1,0:T(8,128)} %conductance.1, bf16[1,2,128,128]{3,2,1,0:T(8,128)(2,1)} %inverse.1), custom_call_target="tpu_custom_call" | custom-call | tf_op jit(solution)/shard_map/pallas_call | solution.py:623
  51.1 1.9 %copy.5 = f32[16,32,256]{2,1,0:T(8,128)} copy(f32[16,32,256]{2,1,0:T(8,128)} %shard_map.37) | data formatting | bytes 1048576

commit v3 on v2

v3 whole, which is shorter than its diff:
```python
import functools
import math

import jax
import jax.numpy as jnp
from jax import lax
from jax.experimental import pallas as pl
from jax.experimental.pallas import tpu as pltpu
from jax.sharding import PartitionSpec as P

MESH = pl.DeviceIdType.MESH

LMAX = 2.0
LMIN = 0.25
THETA = 0.5 * (LMAX + LMIN)
DELTA = 0.5 * (LMAX - LMIN)
SIGMA = THETA / DELTA
RATIO_0 = 1.0 / SIGMA
RATIO_1 = 1.0 / (2.0 * SIGMA - RATIO_0)
RATIO_2 = 1.0 / (2.0 * SIGMA - RATIO_1)
STEP_1 = (RATIO_1 * RATIO_0, 2.0 * RATIO_1 / DELTA)
STEP_2 = (RATIO_2 * RATIO_1, 2.0 * RATIO_2 / DELTA)

F32 = jnp.float32
BF16 = jnp.bfloat16

EXCHANGES = (
    "fine", "kappa_1", "kappa_2", "matrix", "source_1", "smooth_0", "source_2", "gather", "smooth_2", "coarse",
)
AROUND = [(a, b) for a in (-1, 0, 1) for b in (-1, 0, 1) if (a, b) != (0, 0)]
WIDE = [(a, b) for a in (-2, -1, 0, 1, 2) for b in (-1, 0, 1) if (a, b) != (0, 0)]


class Level:
    def __init__(self, nx, ny, x0, side, R, J, hold, row0, erow, xc, coarse, most):
        self.nx, self.ny, self.X, self.x0, self.side = nx, ny, nx + 2 * x0, x0, side
        self.R, self.J, self.hold, self.row0, self.most = R, J, hold, row0, most
        self.erow, self.xc, self.coarse = erow, xc, coarse
        self.rows = ny + 2 * side

    def scratch(self):
        X, R, J = self.X, self.R, self.J
        vm = lambda *shape: pltpu.VMEM(shape + (128,), F32)
        blocked = {name: vm(X, R, J, 8) for name in ("CM", "CP", "Q", "G", "D", "DIR")}
        natural = {name: vm(X, R, self.rows) for name in ("NS", "NK", "RN")}
        return dict(
            E=vm(self.coarse[0], R, self.coarse[1]),
            HK=vm(X, R, J + 2, 8),
            CX=vm(X + 1, R, J, 8),
            CY=vm(X, R, J + 1, 8),
            VA=vm(X, R, J + 2, 8),
            VB=vm(X, R, J + 2, 8),
            **blocked,
            **natural,
        )


LEVELS = (
    Level(16, 32, 4, 8, 2, 5, 1, 4, 20, 8, (28, 80), 6),
    Level(8, 16, 10, 16, 1, 5, 1, 4, 4, 3, (20, 48), 12),
    Level(4, 8, 8, 8, 1, 3, 2, 0, 0, 0, (10, 24), 16),
)


def lanes(*lead):
    return lax.broadcasted_iota(jnp.int32, lead + (8, 128), len(lead) + 1)


def sublanes():
    return lax.broadcasted_iota(jnp.int32, (8, 128), 0)


def turn(value, shift, axis):
    return pltpu.roll(value, shift % value.shape[axis], axis)


def pick(value, index):
    return jnp.take_along_axis(value, index, axis=1, mode="promise_in_bounds")


def rows_of(L, j):
    return pl.ds(L.row0 + j, 8, stride=L.J)


def beside_z(L, parts):
    h = L.hold
    down = [turn(p, h, 2) for p in parts]
    up = [turn(p, -h, 2) for p in parts]
    if L.R == 2:
        lane = lanes(L.J)
        down[1] = jnp.where(lane == 0, down[0], down[1])
        up[0] = jnp.where(lane == 127, up[1], up[0])
    return down, up


def store_wrapped(ref, x, r, J, values):
    ref[x, r, 1 : J + 1] = values
    ref[x, r, 0] = turn(values[J - 1], 1, 0)
    ref[x, r, J + 1] = turn(values[0], -1, 0)


def rows_from(L, ref, x, r):
    return jnp.stack([ref[x, r, rows_of(L, j), :] for j in range(L.J)])


def rows_to(L, ref, x, r, values):
    for j in range(L.J):
        ref[x, r, rows_of(L, j), :] = values[j]


def loop(lo, hi, body, most=1):
    count = hi - lo
    steps = -(-count // most)
    U = -(-count // steps)
    whole = count // U
    if whole > 1:

        def step(i, carry):
            body(lo + i * U, U)
            return carry

        lax.fori_loop(0, whole, step, 0)
    elif whole == 1:
        body(lo, U)
    if count > whole * U:
        body(lo + whole * U, count - whole * U)


def prepare(L, M, lo, hi, gx, gy, count_x, count_y):
    J, R, h = L.J, L.R, L.hold
    shape = (J, 8, 128)
    lane = lanes(J)
    place = lax.broadcasted_iota(jnp.int32, shape, 0) + J * lax.broadcasted_iota(jnp.int32, shape, 1)
    place = place + (gy * L.ny - L.side + L.row0)
    keep = jnp.where((place >= 0) & (place < L.ny * count_y), 0.5, 0.0).astype(F32)

    def halves(x, U):
        NK, HK = M["NK"].at[pl.ds(x, U)], M["HK"].at[pl.ds(x, U)]
        for u in range(U):
            place = gx * L.nx + x + u - L.x0
            inside = jnp.where((place >= 0) & (place < L.nx * count_x), 1.0, 0.0).astype(F32)
            mask = keep * inside
            for r in range(R):
                store_wrapped(HK, u, r, J, rows_from(L, NK, u, r) * mask)

    loop(lo - 1, hi + 1, halves, L.most)
    for r in range(R):
        M["CX"][lo, r] = M["HK"][lo - 1, r, 1 : J + 1] + M["HK"][lo, r, 1 : J + 1]

    def couple(x, U):
        HK, CX = M["HK"].at[pl.ds(x - 1, U + 2)], M["CX"].at[pl.ds(x, U + 1)]
        CY, CM, CP, D, Q = (M[name].at[pl.ds(x, U)] for name in ("CY", "CM", "CP", "D", "Q"))
        for u in range(U):
            mine = [HK[u + 1, r, 1 : J + 1] for r in range(R)]
            down, up = beside_z(L, mine)
            down[0] = jnp.where(lane < h, 0.0, down[0])
            up[R - 1] = jnp.where(lane >= 128 - h, 0.0, up[R - 1])
            for r in range(R):
                c = mine[r]
                xm, xp = HK[u, r, 1 : J + 1], HK[u + 2, r, 1 : J + 1]
                ym, yp = HK[u + 1, r, 0:J], HK[u + 1, r, 2 : J + 2]
                diagonal = (xm + xp) + (ym + yp) + (down[r] + up[r]) + 6.0 * c
                CX[u + 1, r] = c + xp
                CY[u, r, 0:J] = c + ym
                CY[u, r, J] = c[J - 1] + yp[J - 1]
                low, high = c + down[r], c + up[r]
                if r == 0:
                    low = jnp.where(lane < h, 0.0, low)
                if r == R - 1:
                    high = jnp.where(lane >= 128 - h, 0.0, high)
                CM[u, r] = low
                CP[u, r] = high
                D[u, r] = diagonal
                Q[u, r] = jnp.where(c > 0.0, 1.0 / diagonal, 0.0)

    loop(lo, hi, couple, L.most)


def scale_source(L, M, name, lo, hi, start):
    J, field = L.J, M[name]

    def body(x, U):
        Q, G, VA, NS = (ref.at[pl.ds(x, U)] for ref in (M["Q"], M["G"], M["VA"], field))
        for u in range(U):
            for r in range(L.R):
                g = Q[u, r] * rows_from(L, NS, u, r)
                G[u, r] = g
                if start:
                    store_wrapped(VA, u, r, J, g * (1.0 / THETA))

    loop(lo, hi, body, L.most)


def sweep(L, M, src, dst, lo, hi, kind, step=None, keep_rows=None, emit=None):
    J, R = L.J, L.R

    def body(x, U):
        V, CX = M[src].at[pl.ds(x - 1, U + 2)], M["CX"].at[pl.ds(x, U + 1)]
        CY, CM, CP, D, Q, G, DIR = (M[name].at[pl.ds(x, U)] for name in ("CY", "CM", "CP", "D", "Q", "G", "DIR"))
        if dst is not None:
            W = M[dst].at[pl.ds(x, U)]
        if kind == "residual":
            RN = M["RN"].at[pl.ds(x, U)]
        if keep_rows is not None:
            kept = keep_rows.at[pl.ds(x - L.x0 + 1, U)]
        for u in range(U):
            mine = [V[u + 1, r, 1 : J + 1] for r in range(R)]
            down, up = beside_z(L, mine)
            new = []
            for r in range(R):
                c = mine[r]
                near = CX[u, r] * V[u, r, 1 : J + 1] + CX[u + 1, r] * V[u + 2, r, 1 : J + 1]
                near = near + (CY[u, r, 0:J] * V[u + 1, r, 0:J] + CY[u, r, 1 : J + 1] * V[u + 1, r, 2 : J + 2])
                near = near + (CM[u, r] * down[r] + CP[u, r] * up[r])
                update = (G[u, r] - c) + Q[u, r] * near
                if kind == "residual":
                    rows_to(L, RN, u, r, D[u, r] * update)
                    continue
                if kind == "first":
                    direction = update * (1.0 / THETA)
                elif kind == "from_zero":
                    direction = step[0] * c + step[1] * update
                else:
                    direction = step[0] * DIR[u, r] + step[1] * update
                if kind != "last":
                    DIR[u, r] = direction
                value = c + direction
                if dst is not None:
                    store_wrapped(W, u, r, J, value)
                if keep_rows is not None:
                    rows_to(L, kept, u, r, value)
                new.append(value)
            if emit is not None:
                emit(x + u, new)

    loop(lo, hi, body, L.most)


def descend(L, M, margin, keep_rows=None):
    lo, hi = L.x0 - margin, L.x0 + L.nx + margin
    sweep(L, M, "VA", "VB", lo - 2, hi + 2, "from_zero", STEP_1)
    sweep(L, M, "VB", "VA", lo - 1, hi + 1, "last", STEP_2, keep_rows=keep_rows)
    sweep(L, M, "VA", None, lo, hi, "residual")


def ascend(L, M, margin, emit, smoothed=None):
    lo, hi = L.x0, L.x0 + L.nx

    def begin(x, U):
        HK, VA = (M[name].at[pl.ds(x, U)] for name in ("HK", "VA"))
        if smoothed is not None:
            NV = smoothed.at[pl.ds(x, U)]
        for u in range(U):
            xc = lax.shift_right_logical(x + u, 1) + L.xc
            for r in range(L.R):
                added = [M["E"][xc, r, pl.ds(L.erow + j, 8, stride=L.J), :] for j in range(L.J)]
                base = VA[u, r, 1 : L.J + 1] if smoothed is None else rows_from(L, NV, u, r)
                inside = HK[u, r, 1 : L.J + 1] > 0.0
                store_wrapped(VA, u, r, L.J, jnp.where(inside, jnp.stack(added) + base, 0.0))

    loop(lo - margin, hi + margin, begin, L.most)
    margin -= 1
    sweep(L, M, "VA", "VB", lo - margin, hi + margin, "first")
    margin -= 1
    sweep(L, M, "VB", "VA", lo - margin, hi + margin, "next", STEP_1)
    margin -= 1
    sweep(L, M, "VA", None, lo - margin, hi + margin, "last", STEP_2, emit=emit)


def coarsen(L, src, row, tiles, scale, put):
    lane = lanes()
    even = (lane * 2) & 127

    def body(x, U):
        pairs = src.at[pl.ds(2 * x, 2 * U)]
        for u, t in [(u, t) for u in range(U) for t in range(tiles)]:
            sums = []
            for r in range(L.R):
                rows = [pairs[2 * u + dx, r, pl.ds(row + 16 * t + b, 8, stride=2), :] for dx in (0, 1) for b in (0, 1)]
                total = (rows[0] + rows[1]) + (rows[2] + rows[3])
                if L.R == 2:
                    sums.append(pick(total + turn(total, -1, 1), even))
                else:
                    other = jnp.where((lane & L.hold) == 0, turn(total, -L.hold, 1), turn(total, L.hold, 1))
                    sums.append(total + other)
            value = jnp.where(lane < 64, sums[0], sums[1]) if L.R == 2 else sums[0]
            put(x + u, t, value * scale)

    return body


def put_rows(dst, dx, row):
    def put(x, t, value):
        dst[dx + x, 0, row + 8 * t : row + 8 * t + 8, :] = value

    return put


def kernel(gx_size, gy_size, names, source, conductance, inverse, out, *refs):
    S = dict(zip(names, refs))
    M = [{k[1:]: v for k, v in S.items() if k[0] == str(l)} for l in range(3)]
    M[2]["s2"] = S["s2"]
    gx, gy = lax.axis_index("gx"), lax.axis_index("gy")
    L0, L1, L2 = LEVELS

    def device(a, b):
        return {"gx": lax.rem(gx + a + gx_size, gx_size), "gy": lax.rem(gy + b + gy_size, gy_size)}

    class Exchange:
        def __init__(self, name):
            self.out, self.back, self.rows, self.copies = S["send_" + name], S["recv_" + name], 0, []

        def add(self, src, dst, a, b):
            copy = pltpu.make_async_remote_copy(
                src_ref=src, dst_ref=dst, send_sem=self.out, recv_sem=self.back, device_id=device(a, b), device_id_type=MESH
            )
            self.copies.append(copy)
            rows = math.prod(src.shape[:-1])
            self.rows += rows if src.dtype == F32 else rows // 2

        def start(self):
            for copy in self.copies:
                copy.start()
            return self

        def wait(self, semaphore):
            size = S["size"].at[pl.ds(0, self.rows)]
            pltpu.make_async_copy(size, size, semaphore).wait()

        def arrive(self):
            self.wait(self.back)

        def left(self):
            self.wait(self.out)

    def exchange(L, src, sx0, dst, near, far, name):
        both = Exchange(name)
        h = L.side
        for a, b in WIDE if far else AROUND:
            w = {0: L.nx, 1: near, 2: far}[abs(a)]
            xs = sx0 + (L.nx - w if a > 0 else 0)
            xd = {0: L.x0, 1: L.x0 - w, 2: L.x0 - L.nx - w, -1: L.x0 + L.nx, -2: L.x0 + 2 * L.nx}[a]
            ys = h + (L.ny - h if b > 0 else 0)
            yd, wy = {0: (h, L.ny), 1: (0, h), -1: (h + L.ny, h)}[b]
            both.add(src.at[pl.ds(xs, w), :, pl.ds(ys, wy), :], dst.at[pl.ds(xd, w), :, pl.ds(yd, wy), :], a, b)
        return both.start()

    peers = list(WIDE) + [(0, b) for b in range(2, gy_size - 1)]
    barrier = pltpu.get_barrier_semaphore()
    for a, b in peers:
        pl.semaphore_signal(barrier, inc=1, device_id=device(a, b), device_id_type=MESH)

    loads = []
    for n, (src, dst) in enumerate(((conductance, M[0]["NK"]), (source, M[0]["NS"]))):
        for r in range(2):
            copy = pltpu.make_async_copy(
                src.at[:, :, pl.ds(128 * r, 128)],
                dst.at[pl.ds(4, 16), r, pl.ds(8, 32), :],
                S["local"].at[2 * n + r],
            )
            copy.start()
            loads.append(copy)
    for copy in loads:
        copy.wait()

    sub, lane = sublanes(), lanes()
    XP, YP, XR, YR = S["xp"], S["yp"], S["xr"], S["yr"]
    fields = (M[0]["NK"], M[0]["NS"])

    def pack_x(i, _):
        for a in range(2):
            for r in range(2):
                XP[0, a, i, r] = fields[a][4 + i, r, 8:40, :].astype(BF16)
                XP[1, a, i, r] = fields[a][16 + i, r, 8:40, :].astype(BF16)

    loop(0, 4, pack_x)

    def pack_y(i, _):
        for a in range(2):
            low, high = [], []
            for d in range(2):
                x = 4 + 2 * i + d
                near, far = fields[a][x, 0, 8:16, :], fields[a][x, 1, 8:16, :]
                low.append(jnp.where(sub < 4, near, turn(far, 4, 0)))
                near, far = fields[a][x, 0, 32:40, :], fields[a][x, 1, 32:40, :]
                high.append(jnp.where(sub < 4, turn(near, 4, 0), far))
            YP[0, a, i] = jnp.concatenate(low, axis=0).astype(BF16)
            YP[1, a, i] = jnp.concatenate(high, axis=0).astype(BF16)

    loop(0, 8, pack_y)

    pl.semaphore_wait(barrier, len(peers))

    fine = Exchange("fine")
    for a, b in AROUND:
        if b == 0:
            fine.add(XP.at[(a + 1) // 2], XR.at[(1 - a) // 2], a, b)
        else:
            xs, xd, wx = {0: (0, 2, 8), 1: (6, 0, 2), -1: (0, 10, 2)}[a]
            fine.add(YP.at[(b + 1) // 2, :, pl.ds(xs, wx)], YR.at[(1 - b) // 2, :, pl.ds(xd, wx)], a, b)
    fine.start()

    def halve(field, packed):
        packed[10:18, 0, 16:32, :] = field[10:18, 0, 16:32, :].astype(BF16)

    def widen(packed, field):
        def whole(x, U):
            for u in range(U):
                field[x + u, 0] = packed[x + u, 0].astype(F32)

        def ends(x, U):
            for u in range(U):
                for rows in (pl.ds(0, 16), pl.ds(32, 16)):
                    field[x + u, 0, rows, :] = packed[x + u, 0, rows, :].astype(F32)

        loop(0, 10, whole, 5)
        loop(10, 18, ends, 8)
        loop(18, 28, whole, 5)

    loop(0, 8, coarsen(L0, M[0]["NK"].at[pl.ds(4, 16)], 8, 2, 0.125, put_rows(M[1]["NK"], 10, 16)), 4)
    halve(M[1]["NK"], S["k1"])
    kappa_1 = exchange(L1, S["k1"], 10, S["k1"], 8, 2, "kappa_1")
    loop(0, 4, coarsen(L1, M[1]["NK"].at[pl.ds(10, 8)], 16, 1, 0.125, put_rows(M[2]["NK"], 8, 8)), 4)
    kappa_2 = exchange(L2, M[2]["NK"], 8, M[2]["NK"], 4, 4, "kappa_2")

    one = lambda mask: jnp.where(mask, 1.0, 0.0).astype(BF16)
    row = lax.broadcasted_iota(jnp.int32, (128, 128), 0)
    column = lax.broadcasted_iota(jnp.int32, (128, 128), 1)
    order = one(row == ((column >> 2) & 1) * 64 + (column >> 3) * 4 + (column & 3))
    for k in range(2):
        S["mp"][128 * k : 128 * (k + 1), :] = jnp.dot(
            inverse[0, k], order, preferred_element_type=F32
        ).astype(BF16)

    row = lax.broadcasted_iota(jnp.int32, (48, 256), 0)
    column = lax.broadcasted_iota(jnp.int32, (48, 256), 1)
    layer = jnp.where(row >= 24, 1, 0)
    row = row - 24 * layer
    half = jnp.where(row >= 12, 1, 0)
    row = row - 12 * half
    base = layer * 128 + half * 64

    def share(d, _):
        chosen = one(column == base + ((row + (4 * d + 60)) & 63))
        S["ms"][d] = jnp.dot(chosen, S["mp"][...], preferred_element_type=F32).astype(BF16)

    loop(0, gy_size, share)
    matrices = Exchange("matrix")
    for n in range(1, gy_size):
        matrices.add(S["ms"].at[lax.rem(gy + n, gy_size)], S["mm"].at[gy], 0, n)
    matrices.start()
    S["mm"][gy] = S["ms"][gy]

    fine.arrive()

    def unpack_x(i, _):
        for a in range(2):
            for r in range(2):
                fields[a][i, r, 8:40, :] = XR[0, a, i, r].astype(F32)
                fields[a][20 + i, r, 8:40, :] = XR[1, a, i, r].astype(F32)

    loop(0, 4, unpack_x)

    def unpack_y(i, _):
        for a in range(2):
            low, high = YR[0, a, i].astype(F32), YR[1, a, i].astype(F32)
            for d in range(2):
                x = 2 * i + d
                part = low[8 * d : 8 * d + 8]
                fields[a][x, 0, 0:8, :] = turn(part, 4, 0)
                fields[a][x, 1, 0:8, :] = part
                part = high[8 * d : 8 * d + 8]
                fields[a][x, 0, 40:48, :] = part
                fields[a][x, 1, 40:48, :] = turn(part, 4, 0)

    loop(0, 12, unpack_y)

    place = (gx, gy, gx_size, gy_size)
    prepare(L0, M[0], 1, 23, *place)
    scale_source(L0, M[0], "NS", 1, 23, True)
    descend(L0, M[0], 0, S["keep0"])
    residual = M[0]["RN"].at[pl.ds(4, 16)]
    loop(0, 8, coarsen(L0, residual, 8, 2, 0.5, put_rows(M[1]["NS"], 10, 16)), 4)
    halve(M[1]["NS"], S["s1"])
    source_1 = exchange(L1, S["s1"], 10, S["s1"], 8, 2, "source_1")
    smooth_0 = exchange(L0, S["keep0"], 1, S["smooth0"], 3, 0, "smooth_0")

    kappa_1.arrive()
    widen(S["k1"], M[1]["NK"])
    prepare(L1, M[1], 1, 27, *place)
    kappa_2.arrive()
    prepare(L2, M[2], 3, 17, *place)
    source_1.arrive()
    widen(S["s1"], M[1]["NS"])
    scale_source(L1, M[1], "NS", 1, 27, True)
    descend(L1, M[1], 6)

    residual = M[1]["RN"].at[pl.ds(4, 20)]
    loop(0, 10, coarsen(L1, residual, 0, 3, 0.5, put_rows(S["s2"], 5, 0)), 5)
    M[2]["NS"][8:12, :, 8:16, :] = S["s2"][8:12, :, 8:16, :]
    source_2 = exchange(L2, M[2]["NS"], 8, M[2]["NS"], 4, 4, "source_2")
    scale_source(L2, M[2], "s2", 5, 15, True)
    descend(L2, M[2], 0, S["keep2"])
    tiles = []
    residual = M[2]["RN"].at[pl.ds(8, 4)]
    loop(0, 2, coarsen(L2, residual, 8, 1, 1.0 / 128.0, lambda x, t, value: tiles.append(value)), 2)
    rounded = jnp.where(sub < 4, tiles[0], turn(tiles[1], 4, 0)).astype(BF16).astype(F32)
    S["mine"][...] = rounded
    gathered = Exchange("gather")
    for n in range(1, gy_size):
        gathered.add(S["mine"], S["all"].at[gy], 0, n)
    gathered.start()
    smooth_2 = exchange(L2, S["keep2"], 1, S["smooth2"], 4, 4, "smooth_2")
    S["all"][gy] = rounded

    kept = []
    for n, (L, src, dst) in enumerate(((L0, S["keep0"], S["smooth0"]), (L2, S["keep2"], S["smooth2"]))):
        copy = pltpu.make_async_copy(
            src.at[pl.ds(1, L.nx), :, pl.ds(8, L.ny), :],
            dst.at[pl.ds(L.x0, L.nx), :, pl.ds(8, L.ny), :],
            S["local"].at[n],
        )
        copy.start()
        kept.append(copy)
    for old in (fine, kappa_1, kappa_2, matrices, source_1, smooth_0, source_2):
        old.left()
    for copy in kept:
        copy.wait()

    source_2.arrive()
    scale_source(L2, M[2], "NS", 3, 17, False)
    matrices.arrive()
    gathered.arrive()
    right = S["all"][...].reshape(gy_size * 8, 128).astype(BF16)
    layer_of = lax.broadcasted_iota(jnp.int32, (24, 128), 1) >> 2

    def solve(d, total):
        product = jnp.dot(S["mm"][d], right, preferred_element_type=F32)
        total = total + jnp.where(layer_of == 2 * d, product[:24], 0.0)
        return total + jnp.where(layer_of == 2 * d + 1, product[24:], 0.0)

    S["corr"][2] = lax.fori_loop(0, gy_size, solve, jnp.zeros((24, 128), F32))
    coarse = Exchange("coarse")
    for a in (-2, -1, 1, 2):
        coarse.add(S["corr"].at[2], S["corr"].at[2 - a], a, 0)
    coarse.start()
    gathered.left()
    smooth_2.left()
    smooth_2.arrive()
    smooth_0.arrive()
    coarse.arrive()

    for slab in range(5):
        for d in range(2):
            for b in range(2):
                M[2]["E"][2 * slab + d, 0, pl.ds(b, 8, stride=2), :] = S["corr"][slab, 12 * d : 12 * d + 8, :]
                M[2]["E"][2 * slab + d, 0, pl.ds(16 + b, 4, stride=2), :] = S["corr"][slab, 12 * d + 8 : 12 * d + 12, :]

    def emit_2(x, new):
        for j in range(L2.J):
            for b in range(2):
                M[1]["E"][x, 0, pl.ds(2 * j + b, 8, stride=2 * L2.J), :] = new[0][j]

    def emit_1(x, new):
        for j in range(L1.J):
            for r in range(2):
                value = pick(new[0][j], (lane >> 1) + 64 * r)
                for b in range(2):
                    M[0]["E"][x, r, pl.ds(2 * j + b, 8, stride=2 * L1.J), :] = value

    def emit_0(x, new):
        for r in range(2):
            for j in range(L0.J):
                S["result"][x - L0.x0, r, rows_of(L0, j), :] = new[r][j]

    ascend(L2, M[2], 6, emit_2, S["smooth2"])
    ascend(L1, M[1], 5, emit_1)
    ascend(L0, M[0], 3, emit_0, S["smooth0"])

    stores = []
    for r in range(2):
        copy = pltpu.make_async_copy(
            S["result"].at[:, r, pl.ds(8, 32), :], out.at[:, :, pl.ds(128 * r, 128)], S["local"].at[r]
        )
        copy.start()
        stores.append(copy)
    coarse.left()
    for copy in stores:
        copy.wait()


def solution(mesh):
    gx_size, gy_size = mesh.shape["gx"], mesh.shape["gy"]
    scratch = {}
    for l, L in enumerate(LEVELS):
        for name, shape in L.scratch().items():
            scratch[str(l) + name] = shape
    scratch["xp"] = pltpu.VMEM((2, 2, 4, 2, 32, 128), BF16)
    scratch["xr"] = pltpu.VMEM((2, 2, 4, 2, 32, 128), BF16)
    scratch["yp"] = pltpu.VMEM((2, 2, 8, 16, 128), BF16)
    scratch["yr"] = pltpu.VMEM((2, 2, 12, 16, 128), BF16)
    scratch["k1"] = pltpu.VMEM((28, 1, 48, 128), BF16)
    scratch["s1"] = pltpu.VMEM((28, 1, 48, 128), BF16)
    scratch["s2"] = pltpu.VMEM((20, 1, 24, 128), F32)
    scratch["keep0"] = pltpu.VMEM((18, 2, 48, 128), F32)
    scratch["smooth0"] = pltpu.VMEM((24, 2, 48, 128), F32)
    scratch["keep2"] = pltpu.VMEM((6, 1, 24, 128), F32)
    scratch["smooth2"] = pltpu.VMEM((20, 1, 24, 128), F32)
    scratch["size"] = pltpu.VMEM((1280, 128), F32)
    scratch["mp"] = pltpu.VMEM((256, 128), BF16)
    scratch["ms"] = pltpu.VMEM((gy_size, 48, 128), BF16)
    scratch["mm"] = pltpu.VMEM((gy_size, 48, 128), BF16)
    scratch["mine"] = pltpu.VMEM((8, 128), F32)
    scratch["all"] = pltpu.VMEM((gy_size, 8, 128), F32)
    scratch["corr"] = pltpu.VMEM((5, 24, 128), F32)
    scratch["result"] = pltpu.VMEM((16, 2, 48, 128), F32)
    scratch["local"] = pltpu.SemaphoreType.DMA((4,))
    for name in EXCHANGES:
        scratch["send_" + name] = pltpu.SemaphoreType.DMA
        scratch["recv_" + name] = pltpu.SemaphoreType.DMA

    def local(pressure_source, conductance, coarse_inverse):
        return pl.pallas_call(
            functools.partial(kernel, gx_size, gy_size, tuple(scratch)),
            out_shape=jax.ShapeDtypeStruct(pressure_source.shape, F32),
            in_specs=[
                pl.BlockSpec(memory_space=pl.ANY),
                pl.BlockSpec(memory_space=pl.ANY),
                pl.BlockSpec(memory_space=pltpu.VMEM),
            ],
            out_specs=pl.BlockSpec(memory_space=pl.ANY),
            scratch_shapes=list(scratch.values()),
            compiler_params=pltpu.CompilerParams(
                collective_id=0, has_side_effects=True, vmem_limit_bytes=56 * 2**20
            ),
        )(pressure_source, conductance, coarse_inverse)

    in_specs = (P("gx", "gy", None), P("gx", "gy", None), P("gx", "gy", None, None))
    return jax.shard_map(local, mesh=mesh, in_specs=in_specs, out_specs=P("gx", "gy", None), check_vma=False)
```

time: 53.2 us -> 48.4 us (0.910)
  Pallas kernels: 51.1 us -> 46.3 us
    pallas_call x1, Pallas kernels: 51.1 us -> 46.3 us  [local(): pl.pallas_call(functools.partial(kernel, gx_size, gy_size, tuple(scratch)...]
where the time goes in v3:
time: 48.4 us; the launch traced here: 48.2 us
  Pallas kernels  46.3 us (96%)
  local copies, waits for them, and re-layouts  1.88 us (4%)
    pallas_call x1, Pallas kernels, local(): pl.pallas_call(functools.partial(kernel, gx_size, gy_size, tuple(scratch)...  46.3 us
    unnamed x1, local copies, waits for them, and re-layouts  1.88 us

profile of v3, /device:TPU:1, one launch (start us, length us, event | category | flops | bytes accessed | tf_op | source)
XLA Modules:
  0.0 48.2 jit_solution(612653688602576508)
XLA Ops:
  0.0 46.3 %shard_map.37 = f32[16,32,256]{2,1,0:T(8,128)} custom-call(f32[16,32,256]{2,1,0:T(8,128)} %source.1, f32[16,32,256]{2,1,0:T(8,128)} %conductance.1, bf16[1,2,128,128]{3,2,1,0:T(8,128)(2,1)} %inverse.1), custom_call_target="tpu_custom_call" | custom-call | tf_op jit(solution)/shard_map/pallas_call | solution.py:623
  46.4 1.9 %copy.5 = f32[16,32,256]{2,1,0:T(8,128)} copy(f32[16,32,256]{2,1,0:T(8,128)} %shard_map.37) | data formatting | bytes 1048576

commit v4 on v3

--- a/solution.py
+++ b/solution.py
@@ -24,9 +24,7 @@
 F32 = jnp.float32
 BF16 = jnp.bfloat16
 
-EXCHANGES = (
-    "fine", "kappa_1", "kappa_2", "matrix", "source_1", "smooth_0", "source_2", "gather", "smooth_2", "coarse",
-)
+EXCHANGES = ("side_k", "side_s", "side_v", "kappa_1", "matrix", "source_1", "gather", "level_2", "coarse")
 AROUND = [(a, b) for a in (-1, 0, 1) for b in (-1, 0, 1) if (a, b) != (0, 0)]
 WIDE = [(a, b) for a in (-2, -1, 0, 1, 2) for b in (-1, 0, 1) if (a, b) != (0, 0)]
 
@@ -56,8 +54,8 @@
 
 
 LEVELS = (
-    Level(16, 32, 4, 8, 2, 5, 1, 4, 20, 8, (28, 80), 6),
-    Level(8, 16, 10, 16, 1, 5, 1, 4, 4, 3, (20, 48), 12),
+    Level(16, 32, 4, 8, 2, 5, 1, 4, 20, 10, (32, 80), 10),
+    Level(8, 16, 12, 16, 1, 5, 1, 4, 4, 2, (20, 48), 12),
     Level(4, 8, 8, 8, 1, 3, 2, 0, 0, 0, (10, 24), 16),
 )
 
@@ -243,7 +241,7 @@
     sweep(L, M, "VA", None, lo, hi, "residual")
 
 
-def ascend(L, M, margin, emit, smoothed=None):
+def ascend(L, M, margin, emit, smoothed=None, pieces=1, after=lambda n: None):
     lo, hi = L.x0, L.x0 + L.nx
 
     def begin(x, U):
@@ -264,7 +262,11 @@
     margin -= 1
     sweep(L, M, "VB", "VA", lo - margin, hi + margin, "next", STEP_1)
     margin -= 1
-    sweep(L, M, "VA", None, lo - margin, hi + margin, "last", STEP_2, emit=emit)
+    width = (hi - lo + 2 * margin) // pieces
+    for n in range(pieces):
+        first = lo - margin + n * width
+        sweep(L, M, "VA", None, first, first + width, "last", STEP_2, emit=emit)
+        after(n)
 
 
 def coarsen(L, src, row, tiles, scale, put):
@@ -350,60 +352,88 @@
     for a, b in peers:
         pl.semaphore_signal(barrier, inc=1, device_id=device(a, b), device_id_type=MESH)
 
-    loads = []
-    for n, (src, dst) in enumerate(((conductance, M[0]["NK"]), (source, M[0]["NS"]))):
+    fields = (M[0]["NK"], M[0]["NS"], S["smooth0"])
+    XP, YP, XR, YR = S["xp"], S["yp"], S["xr"], S["yr"]
+    sub, lane = sublanes(), lanes()
+
+    loads = [pltpu.make_async_copy(inverse, S["inverse"], S["local"].at[4])]
+    for n, src in enumerate((conductance, source)):
         for r in range(2):
-            copy = pltpu.make_async_copy(
-                src.at[:, :, pl.ds(128 * r, 128)],
-                dst.at[pl.ds(4, 16), r, pl.ds(8, 32), :],
-                S["local"].at[2 * n + r],
+            loads.append(
+                pltpu.make_async_copy(
+                    src.at[:, :, pl.ds(128 * r, 128)],
+                    fields[n].at[pl.ds(4, 16), r, pl.ds(8, 32), :],
+                    S["local"].at[2 * n + r],
+                )
             )
-            copy.start()
-            loads.append(copy)
     for copy in loads:
-        copy.wait()
-
-    sub, lane = sublanes(), lanes()
-    XP, YP, XR, YR = S["xp"], S["yp"], S["xr"], S["yr"]
-    fields = (M[0]["NK"], M[0]["NS"])
-
-    def pack_x(i, _):
-        for a in range(2):
+        copy.start()
+
+    def pack(a, field, first):
+        def pack_x(i, _):
             for r in range(2):
-                XP[0, a, i, r] = fields[a][4 + i, r, 8:40, :].astype(BF16)
-                XP[1, a, i, r] = fields[a][16 + i, r, 8:40, :].astype(BF16)
-
-    loop(0, 4, pack_x)
-
-    def pack_y(i, _):
-        for a in range(2):
+                XP[a, 0, i, r] = field[first + i, r, 8:40, :].astype(BF16)
+                XP[a, 1, i, r] = field[first + 12 + i, r, 8:40, :].astype(BF16)
+
+        def pack_y(i, _):
             low, high = [], []
             for d in range(2):
-                x = 4 + 2 * i + d
-                near, far = fields[a][x, 0, 8:16, :], fields[a][x, 1, 8:16, :]
+                x = first + 2 * i + d
+                near, far = field[x, 0, 8:16, :], field[x, 1, 8:16, :]
                 low.append(jnp.where(sub < 4, near, turn(far, 4, 0)))
-                near, far = fields[a][x, 0, 32:40, :], fields[a][x, 1, 32:40, :]
+                near, far = field[x, 0, 32:40, :], field[x, 1, 32:40, :]
                 high.append(jnp.where(sub < 4, turn(near, 4, 0), far))
-            YP[0, a, i] = jnp.concatenate(low, axis=0).astype(BF16)
-            YP[1, a, i] = jnp.concatenate(high, axis=0).astype(BF16)
-
-    loop(0, 8, pack_y)
+            YP[a, 0, i] = jnp.concatenate(low, axis=0).astype(BF16)
+            YP[a, 1, i] = jnp.concatenate(high, axis=0).astype(BF16)
+
+        loop(0, 4, pack_x)
+        loop(0, 8, pack_y)
+
+    def sides(a, name):
+        both = Exchange(name)
+        for x, y in AROUND:
+            if y == 0:
+                both.add(XP.at[a, (x + 1) // 2], XR.at[a, (1 - x) // 2], x, y)
+            else:
+                xs, xd, wx = {0: (0, 2, 8), 1: (6, 0, 2), -1: (0, 10, 2)}[x]
+                both.add(YP.at[a, (y + 1) // 2, pl.ds(xs, wx)], YR.at[a, (1 - y) // 2, pl.ds(xd, wx)], x, y)
+        return both.start()
+
+    def unpack(a):
+        field = fields[a]
+
+        def unpack_x(i, _):
+            for r in range(2):
+                field[i, r, 8:40, :] = XR[a, 0, i, r].astype(F32)
+                field[20 + i, r, 8:40, :] = XR[a, 1, i, r].astype(F32)
+
+        def unpack_y(i, _):
+            low, high = YR[a, 0, i].astype(F32), YR[a, 1, i].astype(F32)
+            for d in range(2):
+                x = 2 * i + d
+                part = low[8 * d : 8 * d + 8]
+                field[x, 0, 0:8, :] = turn(part, 4, 0)
+                field[x, 1, 0:8, :] = part
+                part = high[8 * d : 8 * d + 8]
+                field[x, 0, 40:48, :] = part
+                field[x, 1, 40:48, :] = turn(part, 4, 0)
+
+        loop(0, 4, unpack_x)
+        loop(0, 12, unpack_y)
+
+    for a in range(2):
+        loads[1 + 2 * a].wait()
+        loads[2 + 2 * a].wait()
+        pack(a, fields[a], 4)
 
     pl.semaphore_wait(barrier, len(peers))
-
-    fine = Exchange("fine")
-    for a, b in AROUND:
-        if b == 0:
-            fine.add(XP.at[(a + 1) // 2], XR.at[(1 - a) // 2], a, b)
-        else:
-            xs, xd, wx = {0: (0, 2, 8), 1: (6, 0, 2), -1: (0, 10, 2)}[a]
-            fine.add(YP.at[(b + 1) // 2, :, pl.ds(xs, wx)], YR.at[(1 - b) // 2, :, pl.ds(xd, wx)], a, b)
-    fine.start()
+    side_k = sides(0, "side_k")
+    side_s = sides(1, "side_s")
 
     def halve(field, packed):
-        packed[10:18, 0, 16:32, :] = field[10:18, 0, 16:32, :].astype(BF16)
-
-    def widen(packed, field):
+        packed[12:20, 0, 16:32, :] = field[12:20, 0, 16:32, :].astype(BF16)
+
+    def widen(packed, field, margin):
         def whole(x, U):
             for u in range(U):
                 field[x + u, 0] = packed[x + u, 0].astype(F32)
@@ -413,23 +443,21 @@
                 for rows in (pl.ds(0, 16), pl.ds(32, 16)):
                     field[x + u, 0, rows, :] = packed[x + u, 0, rows, :].astype(F32)
 
-        loop(0, 10, whole, 5)
-        loop(10, 18, ends, 8)
-        loop(18, 28, whole, 5)
-
-    loop(0, 8, coarsen(L0, M[0]["NK"].at[pl.ds(4, 16)], 8, 2, 0.125, put_rows(M[1]["NK"], 10, 16)), 4)
+        loop(12 - margin, 12, whole, 6)
+        loop(12, 20, ends, 8)
+        loop(20, 20 + margin, whole, 6)
+
+    loop(0, 8, coarsen(L0, M[0]["NK"].at[pl.ds(4, 16)], 8, 2, 0.125, put_rows(M[1]["NK"], 12, 16)), 4)
     halve(M[1]["NK"], S["k1"])
-    kappa_1 = exchange(L1, S["k1"], 10, S["k1"], 8, 2, "kappa_1")
-    loop(0, 4, coarsen(L1, M[1]["NK"].at[pl.ds(10, 8)], 16, 1, 0.125, put_rows(M[2]["NK"], 8, 8)), 4)
-    kappa_2 = exchange(L2, M[2]["NK"], 8, M[2]["NK"], 4, 4, "kappa_2")
-
+
+    loads[0].wait()
     one = lambda mask: jnp.where(mask, 1.0, 0.0).astype(BF16)
     row = lax.broadcasted_iota(jnp.int32, (128, 128), 0)
     column = lax.broadcasted_iota(jnp.int32, (128, 128), 1)
     order = one(row == ((column >> 2) & 1) * 64 + (column >> 3) * 4 + (column & 3))
     for k in range(2):
         S["mp"][128 * k : 128 * (k + 1), :] = jnp.dot(
-            inverse[0, k], order, preferred_element_type=F32
+            S["inverse"][0, k], order, preferred_element_type=F32
         ).astype(BF16)
 
     row = lax.broadcasted_iota(jnp.int32, (48, 256), 0)
@@ -445,60 +473,41 @@
         S["ms"][d] = jnp.dot(chosen, S["mp"][...], preferred_element_type=F32).astype(BF16)
 
     loop(0, gy_size, share)
+    kappa_1 = exchange(L1, S["k1"], 12, S["k1"], 8, 4, "kappa_1")
+
+    place = (gx, gy, gx_size, gy_size)
+    side_k.arrive()
+    unpack(0)
+    prepare(L0, M[0], 1, 23, *place)
+    side_s.arrive()
+    unpack(1)
+    scale_source(L0, M[0], "NS", 1, 23, True)
+    descend(L0, M[0], 0, S["keep0"])
+    residual = M[0]["RN"].at[pl.ds(4, 16)]
+    loop(0, 8, coarsen(L0, residual, 8, 2, 0.5, put_rows(M[1]["NS"], 12, 16)), 4)
+    halve(M[1]["NS"], S["s1"])
+    source_1 = exchange(L1, S["s1"], 12, S["s1"], 8, 2, "source_1")
+
+    kappa_1.arrive()
+    widen(S["k1"], M[1]["NK"], 12)
+    prepare(L1, M[1], 3, 29, *place)
+    loop(0, 16, coarsen(L1, M[1]["NK"], 0, 3, 0.125, put_rows(M[2]["NK"], 2, 0)), 8)
+    prepare(L2, M[2], 3, 17, *place)
     matrices = Exchange("matrix")
     for n in range(1, gy_size):
         matrices.add(S["ms"].at[lax.rem(gy + n, gy_size)], S["mm"].at[gy], 0, n)
     matrices.start()
     S["mm"][gy] = S["ms"][gy]
-
-    fine.arrive()
-
-    def unpack_x(i, _):
-        for a in range(2):
-            for r in range(2):
-                fields[a][i, r, 8:40, :] = XR[0, a, i, r].astype(F32)
-                fields[a][20 + i, r, 8:40, :] = XR[1, a, i, r].astype(F32)
-
-    loop(0, 4, unpack_x)
-
-    def unpack_y(i, _):
-        for a in range(2):
-            low, high = YR[0, a, i].astype(F32), YR[1, a, i].astype(F32)
-            for d in range(2):
-                x = 2 * i + d
-                part = low[8 * d : 8 * d + 8]
-                fields[a][x, 0, 0:8, :] = turn(part, 4, 0)
-                fields[a][x, 1, 0:8, :] = part
-                part = high[8 * d : 8 * d + 8]
-                fields[a][x, 0, 40:48, :] = part
-                fields[a][x, 1, 40:48, :] = turn(part, 4, 0)
-
-    loop(0, 12, unpack_y)
-
-    place = (gx, gy, gx_size, gy_size)
-    prepare(L0, M[0], 1, 23, *place)
-    scale_source(L0, M[0], "NS", 1, 23, True)
-    descend(L0, M[0], 0, S["keep0"])
-    residual = M[0]["RN"].at[pl.ds(4, 16)]
-    loop(0, 8, coarsen(L0, residual, 8, 2, 0.5, put_rows(M[1]["NS"], 10, 16)), 4)
-    halve(M[1]["NS"], S["s1"])
-    source_1 = exchange(L1, S["s1"], 10, S["s1"], 8, 2, "source_1")
-    smooth_0 = exchange(L0, S["keep0"], 1, S["smooth0"], 3, 0, "smooth_0")
-
-    kappa_1.arrive()
-    widen(S["k1"], M[1]["NK"])
-    prepare(L1, M[1], 1, 27, *place)
-    kappa_2.arrive()
-    prepare(L2, M[2], 3, 17, *place)
+    pack(2, S["keep0"], 1)
+    side_v = sides(2, "side_v")
+
     source_1.arrive()
-    widen(S["s1"], M[1]["NS"])
-    scale_source(L1, M[1], "NS", 1, 27, True)
+    widen(S["s1"], M[1]["NS"], 10)
+    scale_source(L1, M[1], "NS", 3, 29, True)
     descend(L1, M[1], 6)
 
-    residual = M[1]["RN"].at[pl.ds(4, 20)]
+    residual = M[1]["RN"].at[pl.ds(6, 20)]
     loop(0, 10, coarsen(L1, residual, 0, 3, 0.5, put_rows(S["s2"], 5, 0)), 5)
-    M[2]["NS"][8:12, :, 8:16, :] = S["s2"][8:12, :, 8:16, :]
-    source_2 = exchange(L2, M[2]["NS"], 8, M[2]["NS"], 4, 4, "source_2")
     scale_source(L2, M[2], "s2", 5, 15, True)
     descend(L2, M[2], 0, S["keep2"])
     tiles = []
@@ -510,25 +519,23 @@
     for n in range(1, gy_size):
         gathered.add(S["mine"], S["all"].at[gy], 0, n)
     gathered.start()
-    smooth_2 = exchange(L2, S["keep2"], 1, S["smooth2"], 4, 4, "smooth_2")
+    odd = (lanes(4) & 1) == 1
+    pair = S["pair"]
+    pair[8:12, 0, 8:16, :] = jnp.where(odd, S["keep2"][1:5, 0, 8:16, :], S["s2"][8:12, 0, 8:16, :])
+    level_2 = exchange(L2, pair, 8, pair, 4, 4, "level_2")
     S["all"][gy] = rounded
 
-    kept = []
-    for n, (L, src, dst) in enumerate(((L0, S["keep0"], S["smooth0"]), (L2, S["keep2"], S["smooth2"]))):
-        copy = pltpu.make_async_copy(
-            src.at[pl.ds(1, L.nx), :, pl.ds(8, L.ny), :],
-            dst.at[pl.ds(L.x0, L.nx), :, pl.ds(8, L.ny), :],
-            S["local"].at[n],
-        )
-        copy.start()
-        kept.append(copy)
-    for old in (fine, kappa_1, kappa_2, matrices, source_1, smooth_0, source_2):
+    kept = pltpu.make_async_copy(
+        S["keep0"].at[pl.ds(1, 16), :, pl.ds(8, 32), :],
+        S["smooth0"].at[pl.ds(4, 16), :, pl.ds(8, 32), :],
+        S["local"].at[0],
+    )
+    kept.start()
+    for old in (side_k, side_s, kappa_1, source_1, matrices, side_v):
         old.left()
-    for copy in kept:
-        copy.wait()
-
-    source_2.arrive()
-    scale_source(L2, M[2], "NS", 3, 17, False)
+    side_v.arrive()
+    unpack(2)
+    kept.wait()
     matrices.arrive()
     gathered.arrive()
     right = S["all"][...].reshape(gy_size * 8, 128).astype(BF16)
@@ -545,9 +552,20 @@
         coarse.add(S["corr"].at[2], S["corr"].at[2 - a], a, 0)
     coarse.start()
     gathered.left()
-    smooth_2.left()
-    smooth_2.arrive()
-    smooth_0.arrive()
+    level_2.left()
+    level_2.arrive()
+
+    def part(x, U):
+        for u in range(U):
+            for t in range(3):
+                rows = pl.ds(8 * t, 8)
+                both = pair[x + u, 0, rows, :]
+                second = (lane & 1) == 1
+                M[2]["NS"][x + u, 0, rows, :] = jnp.where(second, turn(both, 1, 1), both)
+                S["smooth2"][x + u, 0, rows, :] = jnp.where(second, both, turn(both, -1, 1))
+
+    loop(2, 18, part, 8)
+    scale_source(L2, M[2], "NS", 3, 17, False)
     coarse.arrive()
 
     for slab in range(5):
@@ -575,15 +593,19 @@
 
     ascend(L2, M[2], 6, emit_2, S["smooth2"])
     ascend(L1, M[1], 5, emit_1)
-    ascend(L0, M[0], 3, emit_0, S["smooth0"])
-
     stores = []
-    for r in range(2):
-        copy = pltpu.make_async_copy(
-            S["result"].at[:, r, pl.ds(8, 32), :], out.at[:, :, pl.ds(128 * r, 128)], S["local"].at[r]
-        )
-        copy.start()
-        stores.append(copy)
+
+    def store(n):
+        for r in range(2):
+            copy = pltpu.make_async_copy(
+                S["result"].at[pl.ds(8 * n, 8), r, pl.ds(8, 32), :],
+                out.at[pl.ds(8 * n, 8), :, pl.ds(128 * r, 128)],
+                S["local"].at[2 * n + r],
+            )
+            copy.start()
+            stores.append(copy)
+
+    ascend(L0, M[0], 3, emit_0, S["smooth0"], 2, store)
     coarse.left()
     for copy in stores:
         copy.wait()
@@ -595,18 +617,20 @@
     for l, L in enumerate(LEVELS):
         for name, shape in L.scratch().items():
             scratch[str(l) + name] = shape
-    scratch["xp"] = pltpu.VMEM((2, 2, 4, 2, 32, 128), BF16)
-    scratch["xr"] = pltpu.VMEM((2, 2, 4, 2, 32, 128), BF16)
-    scratch["yp"] = pltpu.VMEM((2, 2, 8, 16, 128), BF16)
-    scratch["yr"] = pltpu.VMEM((2, 2, 12, 16, 128), BF16)
-    scratch["k1"] = pltpu.VMEM((28, 1, 48, 128), BF16)
-    scratch["s1"] = pltpu.VMEM((28, 1, 48, 128), BF16)
+    scratch["xp"] = pltpu.VMEM((3, 2, 4, 2, 32, 128), BF16)
+    scratch["xr"] = pltpu.VMEM((3, 2, 4, 2, 32, 128), BF16)
+    scratch["yp"] = pltpu.VMEM((3, 2, 8, 16, 128), BF16)
+    scratch["yr"] = pltpu.VMEM((3, 2, 12, 16, 128), BF16)
+    scratch["k1"] = pltpu.VMEM((32, 1, 48, 128), BF16)
+    scratch["s1"] = pltpu.VMEM((32, 1, 48, 128), BF16)
     scratch["s2"] = pltpu.VMEM((20, 1, 24, 128), F32)
     scratch["keep0"] = pltpu.VMEM((18, 2, 48, 128), F32)
     scratch["smooth0"] = pltpu.VMEM((24, 2, 48, 128), F32)
     scratch["keep2"] = pltpu.VMEM((6, 1, 24, 128), F32)
+    scratch["pair"] = pltpu.VMEM((20, 1, 24, 128), F32)
     scratch["smooth2"] = pltpu.VMEM((20, 1, 24, 128), F32)
-    scratch["size"] = pltpu.VMEM((1280, 128), F32)
+    scratch["size"] = pltpu.VMEM((768, 128), F32)
+    scratch["inverse"] = pltpu.VMEM((1, 2, 128, 128), BF16)
     scratch["mp"] = pltpu.VMEM((256, 128), BF16)
     scratch["ms"] = pltpu.VMEM((gy_size, 48, 128), BF16)
     scratch["mm"] = pltpu.VMEM((gy_size, 48, 128), BF16)
@@ -614,7 +638,7 @@
     scratch["all"] = pltpu.VMEM((gy_size, 8, 128), F32)
     scratch["corr"] = pltpu.VMEM((5, 24, 128), F32)
     scratch["result"] = pltpu.VMEM((16, 2, 48, 128), F32)
-    scratch["local"] = pltpu.SemaphoreType.DMA((4,))
+    scratch["local"] = pltpu.SemaphoreType.DMA((5,))
     for name in EXCHANGES:
         scratch["send_" + name] = pltpu.SemaphoreType.DMA
         scratch["recv_" + name] = pltpu.SemaphoreType.DMA
@@ -626,7 +650,7 @@
             in_specs=[
                 pl.BlockSpec(memory_space=pl.ANY),
                 pl.BlockSpec(memory_space=pl.ANY),
-                pl.BlockSpec(memory_space=pltpu.VMEM),
+                pl.BlockSpec(memory_space=pl.ANY),
             ],
             out_specs=pl.BlockSpec(memory_space=pl.ANY),
             scratch_shapes=list(scratch.values()),

time: 48.4 us -> 43.5 us (0.90)
  Pallas kernels: 46.3 us -> 41.4 us
    pallas_call x1, Pallas kernels: 46.3 us -> 41.4 us  [local(): pl.pallas_call(functools.partial(kernel, gx_size, gy_size, tuple(scratch)...]
where the time goes in v4:
time: 43.5 us; the launch traced here: 43.3 us
  Pallas kernels  41.4 us (95%)
  local copies, waits for them, and re-layouts  1.88 us (4%)
    pallas_call x1, Pallas kernels, local(): pl.pallas_call(functools.partial(kernel, gx_size, gy_size, tuple(scratch)...  41.4 us
    unnamed x1, local copies, waits for them, and re-layouts  1.88 us

profile of v4, /device:TPU:1, one launch (start us, length us, event | category | flops | bytes accessed | tf_op | source)
XLA Modules:
  0.0 43.3 jit_solution(15823890156165596896)
XLA Ops:
  0.0 41.4 %shard_map.37 = f32[16,32,256]{2,1,0:T(8,128)} custom-call(f32[16,32,256]{2,1,0:T(8,128)} %source.1, f32[16,32,256]{2,1,0:T(8,128)} %conductance.1, bf16[1,2,128,128]{3,2,1,0:T(8,128)(2,1)} %inverse.1), custom_call_target="tpu_custom_call" | custom-call | tf_op jit(solution)/shard_map/pallas_call | solution.py:647
  41.4 1.9 %copy.5 = f32[16,32,256]{2,1,0:T(8,128)} copy(f32[16,32,256]{2,1,0:T(8,128)} %shard_map.37) | data formatting | bytes 1048576

commit v5 on v4

--- a/solution.py
+++ b/solution.py
@@ -27,6 +27,9 @@
 EXCHANGES = ("side_k", "side_s", "side_v", "kappa_1", "matrix", "source_1", "gather", "level_2", "coarse")
 AROUND = [(a, b) for a in (-1, 0, 1) for b in (-1, 0, 1) if (a, b) != (0, 0)]
 WIDE = [(a, b) for a in (-2, -1, 0, 1, 2) for b in (-1, 0, 1) if (a, b) != (0, 0)]
+AROUND.sort(key=lambda o: -abs(o[0]) - 2 * abs(o[1]))
+WIDE.sort(key=lambda o: -abs(o[0]) - 2 * abs(o[1]))
+LINE = sorted(range(1, 16), key=lambda n: -min(n // 4, 4 - n // 4) - min(n % 4, 4 - n % 4))
 
 
 class Level:
@@ -347,7 +350,7 @@
             both.add(src.at[pl.ds(xs, w), :, pl.ds(ys, wy), :], dst.at[pl.ds(xd, w), :, pl.ds(yd, wy), :], a, b)
         return both.start()
 
-    peers = list(WIDE) + [(0, b) for b in range(2, gy_size - 1)]
+    peers = [(0, b) for b in LINE if 1 < b < gy_size - 1] + WIDE
     barrier = pltpu.get_barrier_semaphore()
     for a, b in peers:
         pl.semaphore_signal(barrier, inc=1, device_id=device(a, b), device_id_type=MESH)
@@ -395,7 +398,8 @@
             if y == 0:
                 both.add(XP.at[a, (x + 1) // 2], XR.at[a, (1 - x) // 2], x, y)
             else:
-                xs, xd, wx = {0: (0, 2, 8), 1: (6, 0, 2), -1: (0, 10, 2)}[x]
+                wx = 8 if x == 0 else 2 if a == 0 else 1
+                xs, xd = {0: (0, 2), 1: (8 - wx, 2 - wx), -1: (0, 10)}[x]
                 both.add(YP.at[a, (y + 1) // 2, pl.ds(xs, wx)], YR.at[a, (1 - y) // 2, pl.ds(xd, wx)], x, y)
         return both.start()
 
@@ -433,19 +437,18 @@
     def halve(field, packed):
         packed[12:20, 0, 16:32, :] = field[12:20, 0, 16:32, :].astype(BF16)
 
-    def widen(packed, field, margin):
-        def whole(x, U):
-            for u in range(U):
-                field[x + u, 0] = packed[x + u, 0].astype(F32)
-
-        def ends(x, U):
-            for u in range(U):
-                for rows in (pl.ds(0, 16), pl.ds(32, 16)):
-                    field[x + u, 0, rows, :] = packed[x + u, 0, rows, :].astype(F32)
-
-        loop(12 - margin, 12, whole, 6)
-        loop(12, 20, ends, 8)
-        loop(20, 20 + margin, whole, 6)
+    def widen(packed, field, margin, beside):
+        def take(parts):
+            def body(x, U):
+                for u in range(U):
+                    for rows in parts:
+                        field[x + u, 0, rows, :] = packed[x + u, 0, rows, :].astype(F32)
+
+            return body
+
+        loop(12 - margin, 12, take(beside), 12)
+        loop(12, 20, take((pl.ds(0, 16), pl.ds(32, 16))), 8)
+        loop(20, 20 + margin, take(beside), 12)
 
     loop(0, 8, coarsen(L0, M[0]["NK"].at[pl.ds(4, 16)], 8, 2, 0.125, put_rows(M[1]["NK"], 12, 16)), 4)
     halve(M[1]["NK"], S["k1"])
@@ -460,19 +463,20 @@
             S["inverse"][0, k], order, preferred_element_type=F32
         ).astype(BF16)
 
-    row = lax.broadcasted_iota(jnp.int32, (48, 256), 0)
-    column = lax.broadcasted_iota(jnp.int32, (48, 256), 1)
+    row = lax.broadcasted_iota(jnp.int32, (4, 48, 256), 1)
+    column = lax.broadcasted_iota(jnp.int32, (4, 48, 256), 2)
     layer = jnp.where(row >= 24, 1, 0)
     row = row - 24 * layer
     half = jnp.where(row >= 12, 1, 0)
-    row = row - 12 * half
+    row = row - 12 * half + 4 * lax.broadcasted_iota(jnp.int32, (4, 48, 256), 0)
     base = layer * 128 + half * 64
 
     def share(d, _):
-        chosen = one(column == base + ((row + (4 * d + 60)) & 63))
-        S["ms"][d] = jnp.dot(chosen, S["mp"][...], preferred_element_type=F32).astype(BF16)
-
-    loop(0, gy_size, share)
+        chosen = one(column == base + ((row + (16 * d + 60)) & 63)).reshape(192, 256)
+        rows = jnp.dot(chosen, S["mp"][...], preferred_element_type=F32)
+        S["ms"][pl.ds(4 * d, 4)] = rows.astype(BF16).reshape(4, 48, 128)
+
+    loop(0, gy_size // 4, share)
     kappa_1 = exchange(L1, S["k1"], 12, S["k1"], 8, 4, "kappa_1")
 
     place = (gx, gy, gx_size, gy_size)
@@ -486,15 +490,30 @@
     residual = M[0]["RN"].at[pl.ds(4, 16)]
     loop(0, 8, coarsen(L0, residual, 8, 2, 0.5, put_rows(M[1]["NS"], 12, 16)), 4)
     halve(M[1]["NS"], S["s1"])
-    source_1 = exchange(L1, S["s1"], 12, S["s1"], 8, 2, "source_1")
+    for i in range(4):
+        for side in range(2):
+            rows = pl.ds(16 + 8 * side, 8)
+            both = [M[1]["NS"][12 + 2 * i + d, 0, rows, :] for d in range(2)]
+            S["cp"][side, i] = jnp.concatenate(both, axis=0).astype(BF16)
+    source_1 = Exchange("source_1")
+    for a in (-1, 1):
+        for b in (-1, 1):
+            source_1.add(S["cp"].at[(b + 1) // 2], S["cr"].at[(1 - b) // 2, (1 - a) // 2], a, b)
+    own = pl.ds(16, 16)
+    for a, xs, xd, w in ((-2, 12, 28, 1), (2, 19, 3, 1), (-1, 12, 20, 8), (1, 12, 4, 8)):
+        source_1.add(S["s1"].at[pl.ds(xs, w), :, own, :], S["s1"].at[pl.ds(xd, w), :, own, :], a, 0)
+    own = S["s1"].at[pl.ds(12, 8), :, pl.ds(16, 16), :]
+    for b in (-1, 1):
+        source_1.add(own, S["s1"].at[pl.ds(12, 8), :, pl.ds(16 - 16 * b, 16), :], 0, b)
+    source_1.start()
 
     kappa_1.arrive()
-    widen(S["k1"], M[1]["NK"], 12)
+    widen(S["k1"], M[1]["NK"], 12, (pl.ds(0, 48),))
     prepare(L1, M[1], 3, 29, *place)
     loop(0, 16, coarsen(L1, M[1]["NK"], 0, 3, 0.125, put_rows(M[2]["NK"], 2, 0)), 8)
     prepare(L2, M[2], 3, 17, *place)
     matrices = Exchange("matrix")
-    for n in range(1, gy_size):
+    for n in LINE:
         matrices.add(S["ms"].at[lax.rem(gy + n, gy_size)], S["mm"].at[gy], 0, n)
     matrices.start()
     S["mm"][gy] = S["ms"][gy]
@@ -502,7 +521,13 @@
     side_v = sides(2, "side_v")
 
     source_1.arrive()
-    widen(S["s1"], M[1]["NS"], 10)
+    widen(S["s1"], M[1]["NS"], 9, (pl.ds(16, 16),))
+    for i in range(4):
+        for ys in range(2):
+            for xs in range(2):
+                both = S["cr"][ys, xs, i].astype(F32)
+                for d in range(2):
+                    M[1]["NS"][4 + 16 * xs + 2 * i + d, 0, pl.ds(8 + 24 * ys, 8), :] = both[8 * d : 8 * d + 8]
     scale_source(L1, M[1], "NS", 3, 29, True)
     descend(L1, M[1], 6)
 
@@ -516,7 +541,7 @@
     rounded = jnp.where(sub < 4, tiles[0], turn(tiles[1], 4, 0)).astype(BF16).astype(F32)
     S["mine"][...] = rounded
     gathered = Exchange("gather")
-    for n in range(1, gy_size):
+    for n in LINE:
         gathered.add(S["mine"], S["all"].at[gy], 0, n)
     gathered.start()
     odd = (lanes(4) & 1) == 1
@@ -539,14 +564,12 @@
     matrices.arrive()
     gathered.arrive()
     right = S["all"][...].reshape(gy_size * 8, 128).astype(BF16)
+    product = jnp.dot(S["mm"][...].reshape(gy_size * 48, 128), right, preferred_element_type=F32)
     layer_of = lax.broadcasted_iota(jnp.int32, (24, 128), 1) >> 2
-
-    def solve(d, total):
-        product = jnp.dot(S["mm"][d], right, preferred_element_type=F32)
-        total = total + jnp.where(layer_of == 2 * d, product[:24], 0.0)
-        return total + jnp.where(layer_of == 2 * d + 1, product[24:], 0.0)
-
-    S["corr"][2] = lax.fori_loop(0, gy_size, solve, jnp.zeros((24, 128), F32))
+    terms = [jnp.where(layer_of == k, product[24 * k : 24 * k + 24], 0.0) for k in range(2 * gy_size)]
+    while len(terms) > 1:
+        terms = [terms[i] + terms[i + 1] for i in range(0, len(terms), 2)]
+    S["corr"][2] = terms[0]
     coarse = Exchange("coarse")
     for a in (-2, -1, 1, 2):
         coarse.add(S["corr"].at[2], S["corr"].at[2 - a], a, 0)
@@ -623,6 +646,8 @@
     scratch["yr"] = pltpu.VMEM((3, 2, 12, 16, 128), BF16)
     scratch["k1"] = pltpu.VMEM((32, 1, 48, 128), BF16)
     scratch["s1"] = pltpu.VMEM((32, 1, 48, 128), BF16)
+    scratch["cp"] = pltpu.VMEM((2, 4, 16, 128), BF16)
+    scratch["cr"] = pltpu.VMEM((2, 2, 4, 16, 128), BF16)
     scratch["s2"] = pltpu.VMEM((20, 1, 24, 128), F32)
     scratch["keep0"] = pltpu.VMEM((18, 2, 48, 128), F32)
     scratch["smooth0"] = pltpu.VMEM((24, 2, 48, 128), F32)
@@ -646,7 +671,7 @@
     def local(pressure_source, conductance, coarse_inverse):
         return pl.pallas_call(
             functools.partial(kernel, gx_size, gy_size, tuple(scratch)),
-            out_shape=jax.ShapeDtypeStruct(pressure_source.shape, F32),
+            out_shape=pltpu.VMEM(pressure_source.shape, F32),
             in_specs=[
                 pl.BlockSpec(memory_space=pl.ANY),
                 pl.BlockSpec(memory_space=pl.ANY),
@@ -655,9 +680,9 @@
             out_specs=pl.BlockSpec(memory_space=pl.ANY),
             scratch_shapes=list(scratch.values()),
             compiler_params=pltpu.CompilerParams(
-                collective_id=0, has_side_effects=True, vmem_limit_bytes=56 * 2**20
+                collective_id=0, has_side_effects=True, vmem_limit_bytes=40 * 2**20
             ),
-        )(pressure_source, conductance, coarse_inverse)
+        )(*(pltpu.with_memory_space_constraint(x, pltpu.HBM) for x in (pressure_source, conductance, coarse_inverse)))
 
     in_specs = (P("gx", "gy", None), P("gx", "gy", None), P("gx", "gy", None, None))
     return jax.shard_map(local, mesh=mesh, in_specs=in_specs, out_specs=P("gx", "gy", None), check_vma=False)

time: 43.5 us -> 39.4 us (0.906)
  Pallas kernels: 41.4 us -> 38.4 us
  local copies, waits for them, and re-layouts: 1.88 us -> 0.8 us
    pallas_call x1, Pallas kernels: 41.4 us -> 38.4 us  [local(): pl.pallas_call(functools.partial(kernel, gx_size, gy_size, tuple(scratch)...]
    unnamed x1, local copies, waits for them, and re-layouts: 1.88 us -> 0.8 us
where the time goes in v5:
time: 39.4 us; the launch traced here: 39.2 us
  Pallas kernels  38.4 us (97%)
  local copies, waits for them, and re-layouts  0.8 us (2%)
    pallas_call x1, Pallas kernels, local(): pl.pallas_call(functools.partial(kernel, gx_size, gy_size, tuple(scratch)...  38.4 us
    unnamed x1, local copies, waits for them, and re-layouts  0.8 us

profile of v5, /device:TPU:1, one launch (start us, length us, event | category | flops | bytes accessed | tf_op | source)
XLA Modules:
  0.0 39.2 jit_solution(3796056864045684699)
XLA Ops:
  0.0 38.4 %shard_map.37 = f32[16,32,256]{2,1,0:T(8,128)S(1)} custom-call(f32[16,32,256]{2,1,0:T(8,128)} %source.1, f32[16,32,256]{2,1,0:T(8,128)} %conductance.1, bf16[1,2,128,128]{3,2,1,0:T(8,128)(2,1)} %inverse.1), custom_call_target="tpu_custom_call" | custom-call | tf_op jit(solution)/shard_map/pallas_call | solution.py:672
  38.4 0.8 %copy.5 = f32[16,32,256]{2,1,0:T(8,128)} copy(f32[16,32,256]{2,1,0:T(8,128)S(1)} %shard_map.37) | data formatting | bytes 1048576

commit v6 on v5

--- a/solution.py
+++ b/solution.py
@@ -350,7 +350,7 @@
             both.add(src.at[pl.ds(xs, w), :, pl.ds(ys, wy), :], dst.at[pl.ds(xd, w), :, pl.ds(yd, wy), :], a, b)
         return both.start()
 
-    peers = [(0, b) for b in LINE if 1 < b < gy_size - 1] + WIDE
+    peers = [(0, b) for b in LINE if 1 < b < gy_size - 1] + AROUND
     barrier = pltpu.get_barrier_semaphore()
     for a, b in peers:
         pl.semaphore_signal(barrier, inc=1, device_id=device(a, b), device_id_type=MESH)
@@ -433,6 +433,8 @@
     pl.semaphore_wait(barrier, len(peers))
     side_k = sides(0, "side_k")
     side_s = sides(1, "side_s")
+    for a in (-1, 1):
+        pl.semaphore_signal(S["ready"], inc=1, device_id=device(a, 0), device_id_type=MESH)
 
     def halve(field, packed):
         packed[12:20, 0, 16:32, :] = field[12:20, 0, 16:32, :].astype(BF16)
@@ -477,6 +479,7 @@
         S["ms"][pl.ds(4 * d, 4)] = rows.astype(BF16).reshape(4, 48, 128)
 
     loop(0, gy_size // 4, share)
+    pl.semaphore_wait(S["ready"], 2)
     kappa_1 = exchange(L1, S["k1"], 12, S["k1"], 8, 4, "kappa_1")
 
     place = (gx, gy, gx_size, gy_size)
@@ -663,6 +666,7 @@
     scratch["all"] = pltpu.VMEM((gy_size, 8, 128), F32)
     scratch["corr"] = pltpu.VMEM((5, 24, 128), F32)
     scratch["result"] = pltpu.VMEM((16, 2, 48, 128), F32)
+    scratch["ready"] = pltpu.SemaphoreType.REGULAR
     scratch["local"] = pltpu.SemaphoreType.DMA((5,))
     for name in EXCHANGES:
         scratch["send_" + name] = pltpu.SemaphoreType.DMA

time: 39.4 us -> 38.2 us (0.970)
  Pallas kernels: 38.4 us -> 37.2 us
    pallas_call x1, Pallas kernels: 38.4 us -> 37.2 us  [local(): pl.pallas_call(functools.partial(kernel, gx_size, gy_size, tuple(scratch)...]
where the time goes in v6:
time: 38.2 us; the launch traced here: 38 us
  Pallas kernels  37.2 us (97%)
  local copies, waits for them, and re-layouts  0.8 us (2%)
    pallas_call x1, Pallas kernels, local(): pl.pallas_call(functools.partial(kernel, gx_size, gy_size, tuple(scratch)...  37.2 us
    unnamed x1, local copies, waits for them, and re-layouts  0.8 us

profile of v6, /device:TPU:1, one launch (start us, length us, event | category | flops | bytes accessed | tf_op | source)
XLA Modules:
  0.0 38.0 jit_solution(2554318739838860599)
XLA Ops:
  0.0 37.2 %shard_map.37 = f32[16,32,256]{2,1,0:T(8,128)S(1)} custom-call(f32[16,32,256]{2,1,0:T(8,128)} %source.1, f32[16,32,256]{2,1,0:T(8,128)} %conductance.1, bf16[1,2,128,128]{3,2,1,0:T(8,128)(2,1)} %inverse.1), custom_call_target="tpu_custom_call" | custom-call | tf_op jit(solution)/shard_map/pallas_call | solution.py:676
  37.2 0.8 %copy.5 = f32[16,32,256]{2,1,0:T(8,128)} copy(f32[16,32,256]{2,1,0:T(8,128)S(1)} %shard_map.37) | data formatting | bytes 1048576

commit v7 on v6

--- a/solution.py
+++ b/solution.py
@@ -42,7 +42,7 @@
     def scratch(self):
         X, R, J = self.X, self.R, self.J
         vm = lambda *shape: pltpu.VMEM(shape + (128,), F32)
-        blocked = {name: vm(X, R, J, 8) for name in ("CM", "CP", "Q", "G", "D", "DIR")}
+        blocked = {name: vm(X, R, J, 8) for name in ("CM", "CP", "Q", "G", "D")}
         natural = {name: vm(X, R, self.rows) for name in ("NS", "NK", "RN")}
         return dict(
             E=vm(self.coarse[0], R, self.coarse[1]),
@@ -57,8 +57,8 @@
 
 
 LEVELS = (
-    Level(16, 32, 4, 8, 2, 5, 1, 4, 20, 10, (32, 80), 10),
-    Level(8, 16, 12, 16, 1, 5, 1, 4, 4, 2, (20, 48), 12),
+    Level(16, 32, 4, 8, 2, 5, 1, 4, 20, 10, (32, 80), 22),
+    Level(8, 16, 12, 16, 1, 5, 1, 4, 4, 2, (20, 48), 26),
     Level(4, 8, 8, 8, 1, 3, 2, 0, 0, 0, (10, 24), 16),
 )
 
@@ -152,14 +152,13 @@
         HK, CX = M["HK"].at[pl.ds(x - 1, U + 2)], M["CX"].at[pl.ds(x, U + 1)]
         CY, CM, CP, D, Q = (M[name].at[pl.ds(x, U)] for name in ("CY", "CM", "CP", "D", "Q"))
         for u in range(U):
-            mine = [HK[u + 1, r, 1 : J + 1] for r in range(R)]
-            down, up = beside_z(L, mine)
+            slabs = [beside_y(L, HK, u + 1, r) for r in range(R)]
+            down, up = beside_z(L, [slab[0] for slab in slabs])
             down[0] = jnp.where(lane < h, 0.0, down[0])
             up[R - 1] = jnp.where(lane >= 128 - h, 0.0, up[R - 1])
             for r in range(R):
-                c = mine[r]
+                c, ym, yp = slabs[r]
                 xm, xp = HK[u, r, 1 : J + 1], HK[u + 2, r, 1 : J + 1]
-                ym, yp = HK[u + 1, r, 0:J], HK[u + 1, r, 2 : J + 2]
                 diagonal = (xm + xp) + (ym + yp) + (down[r] + up[r]) + 6.0 * c
                 CX[u + 1, r] = c + xp
                 CY[u, r, 0:J] = c + ym
@@ -192,41 +191,42 @@
     loop(lo, hi, body, L.most)
 
 
-def sweep(L, M, src, dst, lo, hi, kind, step=None, keep_rows=None, emit=None):
+def beside_y(L, ref, x, r):
+    c = ref[x, r, 1 : L.J + 1]
+    low, high = ref[x, r, 0:1], ref[x, r, L.J + 1 : L.J + 2]
+    return c, jnp.concatenate([low, c[:-1]], axis=0), jnp.concatenate([c[1:], high], axis=0)
+
+
+def sweep(L, M, src, dst, lo, hi, step, keep_rows=None, emit=None):
     J, R = L.J, L.R
 
     def body(x, U):
         V, CX = M[src].at[pl.ds(x - 1, U + 2)], M["CX"].at[pl.ds(x, U + 1)]
-        CY, CM, CP, D, Q, G, DIR = (M[name].at[pl.ds(x, U)] for name in ("CY", "CM", "CP", "D", "Q", "G", "DIR"))
-        if dst is not None:
-            W = M[dst].at[pl.ds(x, U)]
-        if kind == "residual":
+        CY, CM, CP, D, Q, G = (M[name].at[pl.ds(x, U)] for name in ("CY", "CM", "CP", "D", "Q", "G"))
+        W = M[dst].at[pl.ds(x, U)] if dst is not None else None
+        if step is None:
             RN = M["RN"].at[pl.ds(x, U)]
         if keep_rows is not None:
             kept = keep_rows.at[pl.ds(x - L.x0 + 1, U)]
         for u in range(U):
-            mine = [V[u + 1, r, 1 : J + 1] for r in range(R)]
-            down, up = beside_z(L, mine)
+            slabs = [beside_y(L, V, u + 1, r) for r in range(R)]
+            down, up = beside_z(L, [slab[0] for slab in slabs])
             new = []
             for r in range(R):
-                c = mine[r]
+                c, ym, yp = slabs[r]
+                cy = CY[u, r]
                 near = CX[u, r] * V[u, r, 1 : J + 1] + CX[u + 1, r] * V[u + 2, r, 1 : J + 1]
-                near = near + (CY[u, r, 0:J] * V[u + 1, r, 0:J] + CY[u, r, 1 : J + 1] * V[u + 1, r, 2 : J + 2])
+                near = near + (cy[:-1] * ym + cy[1:] * yp)
                 near = near + (CM[u, r] * down[r] + CP[u, r] * up[r])
-                update = (G[u, r] - c) + Q[u, r] * near
-                if kind == "residual":
-                    rows_to(L, RN, u, r, D[u, r] * update)
+                z = G[u, r] + Q[u, r] * near
+                if step is None:
+                    rows_to(L, RN, u, r, D[u, r] * (z - c))
                     continue
-                if kind == "first":
-                    direction = update * (1.0 / THETA)
-                elif kind == "from_zero":
-                    direction = step[0] * c + step[1] * update
-                else:
-                    direction = step[0] * DIR[u, r] + step[1] * update
-                if kind != "last":
-                    DIR[u, r] = direction
-                value = c + direction
-                if dst is not None:
+                a, b, before = step
+                value = (1.0 + a - b) * c + b * z
+                if before:
+                    value = value - a * W[u, r, 1 : J + 1]
+                if emit is None:
                     store_wrapped(W, u, r, J, value)
                 if keep_rows is not None:
                     rows_to(L, kept, u, r, value)
@@ -239,9 +239,9 @@
 
 def descend(L, M, margin, keep_rows=None):
     lo, hi = L.x0 - margin, L.x0 + L.nx + margin
-    sweep(L, M, "VA", "VB", lo - 2, hi + 2, "from_zero", STEP_1)
-    sweep(L, M, "VB", "VA", lo - 1, hi + 1, "last", STEP_2, keep_rows=keep_rows)
-    sweep(L, M, "VA", None, lo, hi, "residual")
+    sweep(L, M, "VA", "VB", lo - 2, hi + 2, STEP_1 + (False,))
+    sweep(L, M, "VB", "VA", lo - 1, hi + 1, STEP_2 + (True,), keep_rows=keep_rows)
+    sweep(L, M, "VA", None, lo, hi, None)
 
 
 def ascend(L, M, margin, emit, smoothed=None, pieces=1, after=lambda n: None):
@@ -261,14 +261,14 @@
 
     loop(lo - margin, hi + margin, begin, L.most)
     margin -= 1
-    sweep(L, M, "VA", "VB", lo - margin, hi + margin, "first")
+    sweep(L, M, "VA", "VB", lo - margin, hi + margin, (0.0, 1.0 / THETA, False))
     margin -= 1
-    sweep(L, M, "VB", "VA", lo - margin, hi + margin, "next", STEP_1)
+    sweep(L, M, "VB", "VA", lo - margin, hi + margin, STEP_1 + (True,))
     margin -= 1
     width = (hi - lo + 2 * margin) // pieces
     for n in range(pieces):
         first = lo - margin + n * width
-        sweep(L, M, "VA", None, first, first + width, "last", STEP_2, emit=emit)
+        sweep(L, M, "VA", "VB", first, first + width, STEP_2 + (True,), emit=emit)
         after(n)
 
 
@@ -491,7 +491,7 @@
     scale_source(L0, M[0], "NS", 1, 23, True)
     descend(L0, M[0], 0, S["keep0"])
     residual = M[0]["RN"].at[pl.ds(4, 16)]
-    loop(0, 8, coarsen(L0, residual, 8, 2, 0.5, put_rows(M[1]["NS"], 12, 16)), 4)
+    loop(0, 8, coarsen(L0, residual, 8, 2, 0.5, put_rows(M[1]["NS"], 12, 16)), 8)
     halve(M[1]["NS"], S["s1"])
     for i in range(4):
         for side in range(2):
@@ -535,7 +535,7 @@
     descend(L1, M[1], 6)
 
     residual = M[1]["RN"].at[pl.ds(6, 20)]
-    loop(0, 10, coarsen(L1, residual, 0, 3, 0.5, put_rows(S["s2"], 5, 0)), 5)
+    loop(0, 10, coarsen(L1, residual, 0, 3, 0.5, put_rows(S["s2"], 5, 0)), 10)
     scale_source(L2, M[2], "s2", 5, 15, True)
     descend(L2, M[2], 0, S["keep2"])
     tiles = []

time: 38.2 us -> 35.4 us (0.927)
  Pallas kernels: 37.2 us -> 34.5 us
    pallas_call x1, Pallas kernels: 37.2 us -> 34.5 us  [local(): pl.pallas_call(functools.partial(kernel, gx_size, gy_size, tuple(scratch)...]
where the time goes in v7:
time: 35.4 us; the launch traced here: 35.3 us
  Pallas kernels  34.5 us (97%)
  local copies, waits for them, and re-layouts  0.8 us (2%)
    pallas_call x1, Pallas kernels, local(): pl.pallas_call(functools.partial(kernel, gx_size, gy_size, tuple(scratch)...  34.5 us
    unnamed x1, local copies, waits for them, and re-layouts  0.8 us

profile of v7, /device:TPU:1, one launch (start us, length us, event | category | flops | bytes accessed | tf_op | source)
XLA Modules:
  0.0 35.3 jit_solution(268684742312157806)
XLA Ops:
  0.0 34.5 %shard_map.37 = f32[16,32,256]{2,1,0:T(8,128)S(1)} custom-call(f32[16,32,256]{2,1,0:T(8,128)} %source.1, f32[16,32,256]{2,1,0:T(8,128)} %conductance.1, bf16[1,2,128,128]{3,2,1,0:T(8,128)(2,1)} %inverse.1), custom_call_target="tpu_custom_call" | custom-call | tf_op jit(solution)/shard_map/pallas_call | solution.py:676
  34.5 0.8 %copy.5 = f32[16,32,256]{2,1,0:T(8,128)} copy(f32[16,32,256]{2,1,0:T(8,128)S(1)} %shard_map.37) | data formatting | bytes 1048576

commit v8 on v7

--- a/solution.py
+++ b/solution.py
@@ -605,12 +605,14 @@
             for b in range(2):
                 M[1]["E"][x, 0, pl.ds(2 * j + b, 8, stride=2 * L2.J), :] = new[0][j]
 
-    def emit_1(x, new):
-        for j in range(L1.J):
-            for r in range(2):
-                value = pick(new[0][j], (lane >> 1) + 64 * r)
-                for b in range(2):
-                    M[0]["E"][x, r, pl.ds(2 * j + b, 8, stride=2 * L1.J), :] = value
+    def spread():
+        for r in range(2):
+            half = (lane >> 1) + 64 * r
+            for x in range(L1.x0 - 2, L1.x0 + L1.nx + 2):
+                for j in range(L1.J):
+                    value = pick(M[1]["VB"][x, 0, j + 1], half)
+                    for b in range(2):
+                        M[0]["E"][x, r, pl.ds(2 * j + b, 8, stride=2 * L1.J), :] = value
 
     def emit_0(x, new):
         for r in range(2):
@@ -618,7 +620,8 @@
                 S["result"][x - L0.x0, r, rows_of(L0, j), :] = new[r][j]
 
     ascend(L2, M[2], 6, emit_2, S["smooth2"])
-    ascend(L1, M[1], 5, emit_1)
+    ascend(L1, M[1], 5, None)
+    spread()
     stores = []
 
     def store(n):

time: 35.4 us -> 34.5 us (0.975)
  Pallas kernels: 34.5 us -> 33.5 us
    pallas_call x1, Pallas kernels: 34.5 us -> 33.5 us  [local(): pl.pallas_call(functools.partial(kernel, gx_size, gy_size, tuple(scratch)...]
where the time goes in v8:
time: 34.5 us; the launch traced here: 34.3 us
  Pallas kernels  33.5 us (97%)
  local copies, waits for them, and re-layouts  0.8 us (2%)
    pallas_call x1, Pallas kernels, local(): pl.pallas_call(functools.partial(kernel, gx_size, gy_size, tuple(scratch)...  33.5 us
    unnamed x1, local copies, waits for them, and re-layouts  0.8 us

profile of v8, /device:TPU:1, one launch (start us, length us, event | category | flops | bytes accessed | tf_op | source)
XLA Modules:
  0.0 34.3 jit_solution(2153228979006509214)
XLA Ops:
  0.0 33.5 %shard_map.37 = f32[16,32,256]{2,1,0:T(8,128)S(1)} custom-call(f32[16,32,256]{2,1,0:T(8,128)} %source.1, f32[16,32,256]{2,1,0:T(8,128)} %conductance.1, bf16[1,2,128,128]{3,2,1,0:T(8,128)(2,1)} %inverse.1), custom_call_target="tpu_custom_call" | custom-call | tf_op jit(solution)/shard_map/pallas_call | solution.py:679
  33.5 0.8 %copy.5 = f32[16,32,256]{2,1,0:T(8,128)} copy(f32[16,32,256]{2,1,0:T(8,128)S(1)} %shard_map.37) | data formatting | bytes 1048576

commit v9 on v8

--- a/solution.py
+++ b/solution.py
@@ -42,13 +42,14 @@
     def scratch(self):
         X, R, J = self.X, self.R, self.J
         vm = lambda *shape: pltpu.VMEM(shape + (128,), F32)
-        blocked = {name: vm(X, R, J, 8) for name in ("CM", "CP", "Q", "G", "D")}
+        blocked = {name: vm(X, R, J, 8) for name in ("CM", "CP", "Q", "D")}
         natural = {name: vm(X, R, self.rows) for name in ("NS", "NK", "RN")}
         return dict(
             E=vm(self.coarse[0], R, self.coarse[1]),
             HK=vm(X, R, J + 2, 8),
             CX=vm(X + 1, R, J, 8),
             CY=vm(X, R, J + 1, 8),
+            G=vm(X, R, J + 2, 8),
             VA=vm(X, R, J + 2, 8),
             VB=vm(X, R, J + 2, 8),
             **blocked,
@@ -176,17 +177,14 @@
     loop(lo, hi, couple, L.most)
 
 
-def scale_source(L, M, name, lo, hi, start):
-    J, field = L.J, M[name]
+def scale_source(L, M, name, lo, hi):
+    field = M[name]
 
     def body(x, U):
-        Q, G, VA, NS = (ref.at[pl.ds(x, U)] for ref in (M["Q"], M["G"], M["VA"], field))
+        Q, G, NS = (ref.at[pl.ds(x, U)] for ref in (M["Q"], M["G"], field))
         for u in range(U):
             for r in range(L.R):
-                g = Q[u, r] * rows_from(L, NS, u, r)
-                G[u, r] = g
-                if start:
-                    store_wrapped(VA, u, r, J, g * (1.0 / THETA))
+                store_wrapped(G, u, r, L.J, Q[u, r] * rows_from(L, NS, u, r))
 
     loop(lo, hi, body, L.most)
 
@@ -202,7 +200,7 @@
 
     def body(x, U):
         V, CX = M[src].at[pl.ds(x - 1, U + 2)], M["CX"].at[pl.ds(x, U + 1)]
-        CY, CM, CP, D, Q, G = (M[name].at[pl.ds(x, U)] for name in ("CY", "CM", "CP", "D", "Q", "G"))
+        CY, CM, CP, D, Q, GW = (M[name].at[pl.ds(x, U)] for name in ("CY", "CM", "CP", "D", "Q", "G"))
         W = M[dst].at[pl.ds(x, U)] if dst is not None else None
         if step is None:
             RN = M["RN"].at[pl.ds(x, U)]
@@ -218,14 +216,19 @@
                 near = CX[u, r] * V[u, r, 1 : J + 1] + CX[u + 1, r] * V[u + 2, r, 1 : J + 1]
                 near = near + (cy[:-1] * ym + cy[1:] * yp)
                 near = near + (CM[u, r] * down[r] + CP[u, r] * up[r])
-                z = G[u, r] + Q[u, r] * near
+                near = Q[u, r] * near
                 if step is None:
-                    rows_to(L, RN, u, r, D[u, r] * (z - c))
+                    rows_to(L, RN, u, r, D[u, r] * (GW[u, r, 1 : J + 1] + near - c))
                     continue
-                a, b, before = step
-                value = (1.0 + a - b) * c + b * z
-                if before:
-                    value = value - a * W[u, r, 1 : J + 1]
+                p, g, scale, before = step
+                if g == scale:
+                    value = p * c + scale * (GW[u, r, 1 : J + 1] + near)
+                elif g == 0.0:
+                    value = p * c + scale * near
+                else:
+                    value = p * c + g * GW[u, r, 1 : J + 1] + scale * near
+                if before != 0.0:
+                    value = value - before * W[u, r, 1 : J + 1]
                 if emit is None:
                     store_wrapped(W, u, r, J, value)
                 if keep_rows is not None:
@@ -237,10 +240,16 @@
     loop(lo, hi, body, L.most)
 
 
+def next_step(step):
+    a, b = step
+    return (1.0 + a - b, b, b, a)
+
+
 def descend(L, M, margin, keep_rows=None):
     lo, hi = L.x0 - margin, L.x0 + L.nx + margin
-    sweep(L, M, "VA", "VB", lo - 2, hi + 2, STEP_1 + (False,))
-    sweep(L, M, "VB", "VA", lo - 1, hi + 1, STEP_2 + (True,), keep_rows=keep_rows)
+    (a, b), (c, d) = STEP_1, STEP_2
+    sweep(L, M, "G", "VB", lo - 2, hi + 2, ((1.0 + a - b) / THETA + b, 0.0, b / THETA, 0.0))
+    sweep(L, M, "VB", "VA", lo - 1, hi + 1, (1.0 + c - d, d - c / THETA, d, 0.0), keep_rows=keep_rows)
     sweep(L, M, "VA", None, lo, hi, None)
 
 
@@ -261,14 +270,14 @@
 
     loop(lo - margin, hi + margin, begin, L.most)
     margin -= 1
-    sweep(L, M, "VA", "VB", lo - margin, hi + margin, (0.0, 1.0 / THETA, False))
+    sweep(L, M, "VA", "VB", lo - margin, hi + margin, (1.0 - 1.0 / THETA, 1.0 / THETA, 1.0 / THETA, 0.0))
     margin -= 1
-    sweep(L, M, "VB", "VA", lo - margin, hi + margin, STEP_1 + (True,))
+    sweep(L, M, "VB", "VA", lo - margin, hi + margin, next_step(STEP_1))
     margin -= 1
     width = (hi - lo + 2 * margin) // pieces
     for n in range(pieces):
         first = lo - margin + n * width
-        sweep(L, M, "VA", "VB", first, first + width, STEP_2 + (True,), emit=emit)
+        sweep(L, M, "VA", "VB", first, first + width, next_step(STEP_2), emit=emit)
         after(n)
 
 
@@ -488,7 +497,7 @@
     prepare(L0, M[0], 1, 23, *place)
     side_s.arrive()
     unpack(1)
-    scale_source(L0, M[0], "NS", 1, 23, True)
+    scale_source(L0, M[0], "NS", 1, 23)
     descend(L0, M[0], 0, S["keep0"])
     residual = M[0]["RN"].at[pl.ds(4, 16)]
     loop(0, 8, coarsen(L0, residual, 8, 2, 0.5, put_rows(M[1]["NS"], 12, 16)), 8)
@@ -502,12 +511,12 @@
     for a in (-1, 1):
         for b in (-1, 1):
             source_1.add(S["cp"].at[(b + 1) // 2], S["cr"].at[(1 - b) // 2, (1 - a) // 2], a, b)
+    own = S["s1"].at[pl.ds(12, 8), :, pl.ds(16, 16), :]
+    for b in (-1, 1):
+        source_1.add(own, S["s1"].at[pl.ds(12, 8), :, pl.ds(16 - 16 * b, 16), :], 0, b)
     own = pl.ds(16, 16)
     for a, xs, xd, w in ((-2, 12, 28, 1), (2, 19, 3, 1), (-1, 12, 20, 8), (1, 12, 4, 8)):
         source_1.add(S["s1"].at[pl.ds(xs, w), :, own, :], S["s1"].at[pl.ds(xd, w), :, own, :], a, 0)
-    own = S["s1"].at[pl.ds(12, 8), :, pl.ds(16, 16), :]
-    for b in (-1, 1):
-        source_1.add(own, S["s1"].at[pl.ds(12, 8), :, pl.ds(16 - 16 * b, 16), :], 0, b)
     source_1.start()
 
     kappa_1.arrive()
@@ -531,12 +540,12 @@
                 both = S["cr"][ys, xs, i].astype(F32)
                 for d in range(2):
                     M[1]["NS"][4 + 16 * xs + 2 * i + d, 0, pl.ds(8 + 24 * ys, 8), :] = both[8 * d : 8 * d + 8]
-    scale_source(L1, M[1], "NS", 3, 29, True)
+    scale_source(L1, M[1], "NS", 3, 29)
     descend(L1, M[1], 6)
 
     residual = M[1]["RN"].at[pl.ds(6, 20)]
     loop(0, 10, coarsen(L1, residual, 0, 3, 0.5, put_rows(S["s2"], 5, 0)), 10)
-    scale_source(L2, M[2], "s2", 5, 15, True)
+    scale_source(L2, M[2], "s2", 5, 15)
     descend(L2, M[2], 0, S["keep2"])
     tiles = []
     residual = M[2]["RN"].at[pl.ds(8, 4)]
@@ -591,7 +600,7 @@
                 S["smooth2"][x + u, 0, rows, :] = jnp.where(second, both, turn(both, -1, 1))
 
     loop(2, 18, part, 8)
-    scale_source(L2, M[2], "NS", 3, 17, False)
+    scale_source(L2, M[2], "NS", 3, 17)
     coarse.arrive()
 
     for slab in range(5):
@@ -622,22 +631,13 @@
     ascend(L2, M[2], 6, emit_2, S["smooth2"])
     ascend(L1, M[1], 5, None)
     spread()
-    stores = []
-
     def store(n):
-        for r in range(2):
-            copy = pltpu.make_async_copy(
-                S["result"].at[pl.ds(8 * n, 8), r, pl.ds(8, 32), :],
-                out.at[pl.ds(8 * n, 8), :, pl.ds(128 * r, 128)],
-                S["local"].at[2 * n + r],
-            )
-            copy.start()
-            stores.append(copy)
+        for x in range(8 * n, 8 * n + 8):
+            for r in range(2):
+                out[x, :, 128 * r : 128 * r + 128] = S["result"][x, r, 8:40, :]
 
     ascend(L0, M[0], 3, emit_0, S["smooth0"], 2, store)
     coarse.left()
-    for copy in stores:
-        copy.wait()
 
 
 def solution(mesh):
@@ -684,7 +684,7 @@
                 pl.BlockSpec(memory_space=pl.ANY),
                 pl.BlockSpec(memory_space=pl.ANY),
             ],
-            out_specs=pl.BlockSpec(memory_space=pl.ANY),
+            out_specs=pl.BlockSpec(memory_space=pltpu.VMEM),
             scratch_shapes=list(scratch.values()),
             compiler_params=pltpu.CompilerParams(
                 collective_id=0, has_side_effects=True, vmem_limit_bytes=40 * 2**20

time: 34.5 us -> 34.3 us (level)
    pallas_call x1, Pallas kernels: 33.5 us -> 33.2 us  [local(): pl.pallas_call(functools.partial(kernel, gx_size, gy_size, tuple(scratch)...]
where the time goes in v9:
time: 34.3 us; the launch traced here: 34 us
  Pallas kernels  33.2 us (97%)
  local copies, waits for them, and re-layouts  0.8 us (2%)
    pallas_call x1, Pallas kernels, local(): pl.pallas_call(functools.partial(kernel, gx_size, gy_size, tuple(scratch)...  33.2 us
    unnamed x1, local copies, waits for them, and re-layouts  0.8 us

profile of v9, /device:TPU:1, one launch (start us, length us, event | category | flops | bytes accessed | tf_op | source)
XLA Modules:
  0.0 34.0 jit_solution(17111100898483174560)
XLA Ops:
  0.0 33.2 %shard_map.37 = f32[16,32,256]{2,1,0:T(8,128)S(1)} custom-call(f32[16,32,256]{2,1,0:T(8,128)} %source.1, f32[16,32,256]{2,1,0:T(8,128)} %conductance.1, bf16[1,2,128,128]{3,2,1,0:T(8,128)(2,1)} %inverse.1), custom_call_target="tpu_custom_call" | custom-call | tf_op jit(solution)/shard_map/pallas_call | solution.py:679
  33.2 0.8 %copy.5 = f32[16,32,256]{2,1,0:T(8,128)} copy(f32[16,32,256]{2,1,0:T(8,128)S(1)} %shard_map.37) | data formatting | bytes 1048576

commit v10 on v9

--- a/solution.py
+++ b/solution.py
@@ -37,7 +37,7 @@
         self.nx, self.ny, self.X, self.x0, self.side = nx, ny, nx + 2 * x0, x0, side
         self.R, self.J, self.hold, self.row0, self.most = R, J, hold, row0, most
         self.erow, self.xc, self.coarse = erow, xc, coarse
-        self.rows = ny + 2 * side
+        self.rows = ny + 2 * side + (8 if R == 1 else 0)
 
     def scratch(self):
         X, R, J = self.X, self.R, self.J
@@ -58,9 +58,9 @@
 
 
 LEVELS = (
-    Level(16, 32, 4, 8, 2, 5, 1, 4, 20, 10, (32, 80), 22),
-    Level(8, 16, 12, 16, 1, 5, 1, 4, 4, 2, (20, 48), 26),
-    Level(4, 8, 8, 8, 1, 3, 2, 0, 0, 0, (10, 24), 16),
+    Level(16, 32, 4, 8, 2, 5, 1, 4, 20, 10, (32, 96), 22),
+    Level(8, 16, 12, 16, 1, 5, 1, 4, 4, 2, (20, 56), 26),
+    Level(4, 8, 8, 8, 1, 3, 2, 0, 0, 0, (10, 32), 16),
 )
 
 
@@ -654,12 +654,12 @@
     scratch["s1"] = pltpu.VMEM((32, 1, 48, 128), BF16)
     scratch["cp"] = pltpu.VMEM((2, 4, 16, 128), BF16)
     scratch["cr"] = pltpu.VMEM((2, 2, 4, 16, 128), BF16)
-    scratch["s2"] = pltpu.VMEM((20, 1, 24, 128), F32)
+    scratch["s2"] = pltpu.VMEM((20, 1, 32, 128), F32)
     scratch["keep0"] = pltpu.VMEM((18, 2, 48, 128), F32)
     scratch["smooth0"] = pltpu.VMEM((24, 2, 48, 128), F32)
-    scratch["keep2"] = pltpu.VMEM((6, 1, 24, 128), F32)
-    scratch["pair"] = pltpu.VMEM((20, 1, 24, 128), F32)
-    scratch["smooth2"] = pltpu.VMEM((20, 1, 24, 128), F32)
+    scratch["keep2"] = pltpu.VMEM((6, 1, 32, 128), F32)
+    scratch["pair"] = pltpu.VMEM((20, 1, 32, 128), F32)
+    scratch["smooth2"] = pltpu.VMEM((20, 1, 32, 128), F32)
     scratch["size"] = pltpu.VMEM((768, 128), F32)
     scratch["inverse"] = pltpu.VMEM((1, 2, 128, 128), BF16)
     scratch["mp"] = pltpu.VMEM((256, 128), BF16)

time: 34.3 us -> 34.3 us (level)
  no operation moved by 1% of the time
where the time goes in v10:
time: 34.3 us; the launch traced here: 34 us
  Pallas kernels  33.2 us (97%)
  local copies, waits for them, and re-layouts  0.8 us (2%)
    pallas_call x1, Pallas kernels, local(): pl.pallas_call(functools.partial(kernel, gx_size, gy_size, tuple(scratch)...  33.2 us
    unnamed x1, local copies, waits for them, and re-layouts  0.8 us

profile of v10, /device:TPU:1, one launch (start us, length us, event | category | flops | bytes accessed | tf_op | source)
XLA Modules:
  0.0 34.0 jit_solution(4492065878783108020)
XLA Ops:
  0.0 33.2 %shard_map.37 = f32[16,32,256]{2,1,0:T(8,128)S(1)} custom-call(f32[16,32,256]{2,1,0:T(8,128)} %source.1, f32[16,32,256]{2,1,0:T(8,128)} %conductance.1, bf16[1,2,128,128]{3,2,1,0:T(8,128)(2,1)} %inverse.1), custom_call_target="tpu_custom_call" | custom-call | tf_op jit(solution)/shard_map/pallas_call | solution.py:679
  33.2 0.8 %copy.5 = f32[16,32,256]{2,1,0:T(8,128)} copy(f32[16,32,256]{2,1,0:T(8,128)S(1)} %shard_map.37) | data formatting | bytes 1048576
